TPU v7x, 32 devices: a whole 2x2x4 slice. The times are simulated.
32 devices in a mesh: table: 8 (over z, core), dp: 4 (over y, x).
Axes of the slice: x: 2, y: 2, z: 4, core: 2. Of those that a mesh axis runs over, the one named last changes fastest.
Arguments:
- ids: int32 [8, 512, 128], P('table', 'dp'), may hold values from 0 to 1023
- mults: int32 [8, 512, 128], P('table', 'dp'), may hold values from 0 to 2
- table: bfloat16 [8192, 128], P('table'), may hold values from -1.25 to 1.25
- user_layer: bfloat16 [1024, 512], replicated, may hold values from -0.1875 to 0.1875
- user_head: bfloat16 [512, 128], replicated, may hold values from -0.25 to 0.25
- item_layer: bfloat16 [1024, 512], replicated, may hold values from -0.1875 to 0.1875
- item_head: bfloat16 [512, 128], replicated, may hold values from -0.25 to 0.25
- counts: int32 [4, 128], P('dp', 'table'), may hold values from 1 to 256
Outputs:
- losses: float32 [4, 128], P('dp', 'table')
- table_change: float32 [8192, 128], P('table')
- user_layer_change: float32 [1024, 512], P('table')
- user_head_change: float32 [512, 128], P('table')
- item_layer_change: float32 [1024, 512], P('table')
- item_head_change: float32 [512, 128], P('table')
All inputs are finite; a program needn't handle non-finite values.
Results may differ from a plain program's by a relative error of at most 0.039.
Values may be sent and summed in bfloat16 or wider, within the bound.
A program may use at most 64 MiB of HBM per device.

v0:
```python
import jax
import jax.numpy as jnp
from jax import lax
from jax.sharding import PartitionSpec as P

LOOKUPS = 8


INVERSE_TEMP = 20.0
EPSILON = 1e-06


def silu_slope(pre):
    gate = jax.nn.sigmoid(pre)
    return gate * (1.0 + pre * (1.0 - gate))


def run_tower(pooled_in, layer, head):
    pre = jnp.dot(pooled_in, layer, preferred_element_type=jnp.float32)
    hidden = jax.nn.silu(pre).astype(jnp.bfloat16)
    output = jnp.dot(hidden, head, preferred_element_type=jnp.float32)
    scale = lax.rsqrt(jnp.sum(output * output, axis=-1, keepdims=True) + EPSILON)
    return (pre, hidden, output * scale, scale)


def tower_back(d_unit, unit, scale, pre, hidden, pooled_in, head):
    along = jnp.sum(unit * d_unit, axis=-1, keepdims=True)
    d_output = ((d_unit - unit * along) * scale).astype(jnp.bfloat16)
    back = lax.dot_general(
        d_output, head, (((1,), (1,)), ((), ())), preferred_element_type=jnp.float32
    )
    d_hidden = (back * silu_slope(pre)).astype(jnp.bfloat16)
    layer_term = lax.dot_general(
        pooled_in, d_hidden, (((0,), (0,)), ((), ())), preferred_element_type=jnp.float32
    )
    head_term = lax.dot_general(
        hidden, d_output, (((0,), (0,)), ((), ())), preferred_element_type=jnp.float32
    )
    return (d_output, d_hidden, layer_term, head_term)


def input_grads(d_hidden, layer):
    return lax.dot_general(
        d_hidden, layer, (((1,), (1,)), ((), ())), preferred_element_type=jnp.float32
    ).astype(jnp.bfloat16)


def shards(ids, mults, table, user_layer, user_head, item_layer, item_head, counts):
    table_count = lax.axis_size("table")
    rows_dev, emb_width = table.shape
    group_rows = ids.shape[1]
    feature_count = ids.shape[2] // LOOKUPS
    own_rows = group_rows // table_count
    user_width = user_layer.shape[0]
    id_blocks = ids[0].reshape(group_rows, feature_count, LOOKUPS).transpose(1, 0, 2)
    mult_blocks = mults[0].reshape(group_rows, feature_count, LOOKUPS).transpose(1, 0, 2)
    table_rows = lax.broadcasted_iota(jnp.int32, (1, rows_dev), 1)

    def lookup_weights(id_block, mult_block):
        running = jnp.zeros((group_rows, rows_dev), jnp.float32)
        for lookup in range(LOOKUPS):
            hit = id_block[:, lookup : lookup + 1] == table_rows
            running = running + jnp.where(
                hit, mult_block[:, lookup : lookup + 1].astype(jnp.float32), 0.0
            )
        return running.astype(jnp.bfloat16)

    def pool_feature(lookup_pair):
        weights = lookup_weights(lookup_pair[0], lookup_pair[1])
        return jnp.dot(weights, table, preferred_element_type=jnp.float32).astype(jnp.bfloat16)

    partial_value = lax.map(pool_feature, (id_blocks, mult_blocks))
    received = lax.all_to_all(partial_value, "table", split_axis=1, concat_axis=1, tiled=True)
    pooled = jnp.sum(
        received.astype(jnp.float32).reshape(feature_count, table_count, own_rows, emb_width),
        axis=1,
    ).astype(jnp.bfloat16)
    pooled = pooled.transpose(1, 0, 2).reshape(own_rows, feature_count * emb_width)
    user_in = pooled[:, :user_width]
    item_in = pooled[:, user_width:]
    user_pre, user_hidden, user_unit, user_scale = run_tower(user_in, user_layer, user_head)
    item_pre, item_hidden, item_unit, item_scale = run_tower(item_in, item_layer, item_head)
    user_vector = user_unit.astype(jnp.bfloat16)
    item_vector = item_unit.astype(jnp.bfloat16)
    item_rows, item_counts = (
        lax.all_gather(item_vector, "dp", axis=0, tiled=True),
        lax.all_gather(counts[0].astype(jnp.bfloat16), "dp", axis=0, tiled=True),
    )
    log_freq = jnp.log(item_counts.astype(jnp.float32))
    scores = (
        INVERSE_TEMP
        * lax.dot_general(
            user_vector, item_rows, (((1,), (1,)), ((), ())), preferred_element_type=jnp.float32
        )
        - log_freq[None, :]
    )
    lse = jnp.log(jnp.sum(jnp.exp(scores), axis=-1))
    own_index = lax.axis_index("dp") * own_rows + lax.broadcasted_iota(jnp.int32, (own_rows,), 0)
    columns = lax.broadcasted_iota(jnp.int32, scores.shape, 1)
    is_positive = columns == own_index[:, None]
    positive = jnp.sum(jnp.where(is_positive, scores, 0.0), axis=-1)
    losses = (lse - positive)[None, :]
    dscore = (jnp.exp(scores - lse[:, None]) - is_positive.astype(jnp.float32)).astype(jnp.bfloat16)
    d_user = INVERSE_TEMP * jnp.dot(dscore, item_rows, preferred_element_type=jnp.float32)
    item_terms = INVERSE_TEMP * lax.dot_general(
        dscore, user_vector, (((0,), (0,)), ((), ())), preferred_element_type=jnp.float32
    )
    d_item = lax.psum_scatter(
        item_terms.astype(jnp.bfloat16), "dp", scatter_dimension=0, tiled=True
    ).astype(jnp.float32)
    user_dout, user_dhid, user_layer_term, user_head_term = tower_back(
        d_user, user_unit, user_scale, user_pre, user_hidden, user_in, user_head
    )
    item_dout, item_dhid, item_layer_term, item_head_term = tower_back(
        d_item, item_unit, item_scale, item_pre, item_hidden, item_in, item_head
    )
    own_grads = jnp.concatenate(
        [input_grads(user_dhid, user_layer), input_grads(item_dhid, item_layer)], axis=1
    )
    group_grads = lax.all_gather(own_grads, "table", axis=0, tiled=True)

    def add_feature(feature, running):
        weights = lookup_weights(id_blocks[feature], mult_blocks[feature])
        column = lax.dynamic_slice_in_dim(group_grads, feature * emb_width, emb_width, 1)
        return running + lax.dot_general(
            weights, column, (((0,), (0,)), ((), ())), preferred_element_type=jnp.float32
        )

    table_part = lax.fori_loop(
        0, feature_count, add_feature, jnp.zeros((rows_dev, emb_width), jnp.float32)
    )
    layer_rows = (
        lax.psum_scatter(
            user_layer_term.astype(jnp.bfloat16), "table", scatter_dimension=0, tiled=True
        ).astype(jnp.float32),
        lax.psum_scatter(
            user_head_term.astype(jnp.bfloat16), "table", scatter_dimension=0, tiled=True
        ).astype(jnp.float32),
        lax.psum_scatter(
            item_layer_term.astype(jnp.bfloat16), "table", scatter_dimension=0, tiled=True
        ).astype(jnp.float32),
        lax.psum_scatter(
            item_head_term.astype(jnp.bfloat16), "table", scatter_dimension=0, tiled=True
        ).astype(jnp.float32),
    )
    totals = (
        lax.psum(table_part.astype(jnp.bfloat16), "dp").astype(jnp.float32),
        lax.psum(layer_rows[0].astype(jnp.bfloat16), "dp").astype(jnp.float32),
        lax.psum(layer_rows[1].astype(jnp.bfloat16), "dp").astype(jnp.float32),
        lax.psum(layer_rows[2].astype(jnp.bfloat16), "dp").astype(jnp.float32),
        lax.psum(layer_rows[3].astype(jnp.bfloat16), "dp").astype(jnp.float32),
    )
    return (losses, totals[0], totals[1], totals[2], totals[3], totals[4])


def solution(mesh):
    in_specs = (
        P("table", "dp", None),
        P("table", "dp", None),
        P("table", None),
        P(),
        P(),
        P(),
        P(),
        P("dp", "table"),
    )
    out_specs = (
        P("dp", "table"),
        P("table", None),
        P("table", None),
        P("table", None),
        P("table", None),
        P("table", None),
    )
    return jax.shard_map(shards, mesh=mesh, in_specs=in_specs, out_specs=out_specs, check_vma=False)
```

profile of v0, /device:TPU:0, one launch (start us, length us, event | category | flops | bytes accessed | tf_op | source)
XLA Modules:
  0.0 273.0 jit_solution(3306158923264824578)
XLA Ops:
  9.2 28.3 %while.27 = (s32[]{:T(128)}, bf16[16,128,128]{2,1,0:T(8,128)(2,1)S(1)}, s32[16,128,8]{1,2,0:T(8,128)S(1)}, s32[16,128,8]{1,2,0:T(8,128)S(1)}, bf16[1024,128]{1,0:T(8,128)(2,1)}, /*index=5*/s32[]{:T(128)}) while((s32[]{:T(128)}, bf16[16,128,128]{2,1,0:T(8,128)(2,1)S(1)}, s32[16,128,8]{1,2,0:T(8,128)S(1)}, ...), condition=%wide.region_1.2_spmd.clone.clone, body=%wide.region_0.1_spmd.clone.clone.sunk | while | flops 36717568 | bytes 335957 | solution.py:72
  9.2 1.7 fusion.84
  11.0 1.7 fusion.84
  12.8 1.7 fusion.84
  25.1 1.7 fusion.84
  26.9 1.7 fusion.84
  28.7 1.7 fusion.84
  30.5 1.7 fusion.84
  32.2 1.7 fusion.84
  34.0 1.7 fusion.84
  35.8 1.7 fusion.84
  38.6 6.5 %all-to-all-start = ((bf16[16,128,128]{2,0,1:T(8,128)(2,1)}), bf16[16,128,128]{2,0,1:T(8,128)(2,1)S(1)}, u32[]{:S(2)}, u32[]{:S(2)}) async-start(bf16[16,128,128]{2,0,1:T(8,128)(2,1)} %copy.20), calls=%async_computation | async-start | bytes 1048576 | tf_op jit(solution)/shard_map/all_to_all | solution.py:73
  47.3 9.9 %all-reduce = bf16[64]{0:T(256)(128)(2,1)S(1)} all-reduce(bf16[64]{0:T(256)(128)(2,1)S(1)} %dynamic-update-slice), channel_id=2, replica_groups=mesh['table'=8,'dp'=4] {'dp'}, use_global_device_ids=true, to_apply=%add | all-reduce | flops 64 | bytes 256
  57.2 3.2 %all-to-all-done = bf16[16,128,128]{2,0,1:T(8,128)(2,1)S(1)} async-done(((bf16[16,128,128]{2,0,1:T(8,128)(2,1)}), bf16[16,128,128]{2,0,1:T(8,128)(2,1)S(1)}, u32[]{:S(2)}, u32[]{:S(2)}) %all-to-all-start) | async-done | bytes 524320 | tf_op jit(solution)/shard_map/all_to_all | solution.py:73
  61.2 8.2 %all_gather.9 = bf16[64,128]{1,0:T(8,128)(2,1)S(1)} all-gather(bf16[16,128]{1,0:T(8,128)(2,1)S(1)} %multiply_convert_fusion.3), channel_id=1, replica_groups=mesh['table'=8,'dp'=4] {'dp'}, dimensions={0}, use_global_device_ids=true | all-gather | bytes 20480 | tf_op jit(solution)/shard_map/all_gather | solution.py:86
  71.0 15.1 %all-reduce.1 = bf16[64,128]{1,0:T(8,128)(2,1)S(1)} all-reduce(bf16[64,128]{1,0:T(8,128)(2,1)S(1)} %fusion.45), channel_id=3, replica_groups=mesh['table'=8,'dp'=4] {'dp'}, use_global_device_ids=true, to_apply=%region_8.9.clone | all-reduce | flops 8192 | bytes 32768
  92.7 16.1 %all_gather.11 = bf16[128,2048]{1,0:T(8,128)(2,1)S(1)} all-gather(bf16[16,2048]{1,0:T(8,128)(2,1)S(1)} %pad_maximum_fusion), channel_id=1, replica_groups=mesh['table'=8,'dp'=4] {'table'}, dimensions={0}, use_global_device_ids=true | all-gather | bytes 589824 | tf_op jit(solution)/shard_map/all_gather | solution.py:120
  108.9 15.2 %while.28 = (s32[]{:T(128)}, f32[1024,128]{1,0:T(8,128)S(1)}, s32[16,128,8]{1,2,0:T(8,128)S(1)}, s32[16,128,8]{1,2,0:T(8,128)S(1)}, bf16[128,2048]{1,0:T(8,128)(...) while((s32[]{:T(128)}, f32[1024,128]{1,0:T(8,128)S(1)}, ...), condition=%wide.region_11.12_spmd.clone.clone, body=%wide.region_10.11_spmd.clone.clone.sunk | while | flops 36963336 | bytes 1122469 | solution.py:129
  124.8 27.5 %reduce-scatter.5.cloned.1.call-done = bf16[128,512]{1,0:T(8,128)(2,1)} async-done(((bf16[1024,512]{1,0:T(8,128)(2,1)}), bf16[128,512]{1,0:T(8,128)(2,1)}) %reduce-scatter.5.cloned.1.call-update) | async-done | bytes 131088 | tf_op jit(solution)/shard_map/reduce_scatter | solution.py:133
  152.3 31.2 %reduce-scatter.11.cloned.1.call-done = bf16[64,128]{1,0:T(8,128)(2,1)} async-done(((bf16[512,128]{1,0:T(8,128)(2,1)}), bf16[64,128]{1,0:T(8,128)(2,1)}) %reduce-scatter.11.cloned.1.call-update) | async-done | bytes 16400 | tf_op jit(solution)/shard_map/reduce_scatter | solution.py:142
  183.5 31.0 %reduce-scatter.7.cloned.1.call-done = bf16[64,128]{1,0:T(8,128)(2,1)} async-done(((bf16[512,128]{1,0:T(8,128)(2,1)}), bf16[64,128]{1,0:T(8,128)(2,1)}) %reduce-scatter.7.cloned.1.call-update) | async-done | bytes 16400 | tf_op jit(solution)/shard_map/reduce_scatter | solution.py:136
  214.5 16.8 %all-reduce.2 = (bf16[64,128]{1,0:T(8,128)(2,1)S(1)}, bf16[64,128]{1,0:T(8,128)(2,1)S(1)}) all-reduce(bf16[64,128]{1,0:T(8,128)(2,1)} %reduce-scatter.7.cloned.1.call-done, bf16[64,128]{1,0:T(8,128)(2,1)} %reduce-scatter.11.cloned.1.call-done), channel_id=1, replica_groups=mesh['table'=8,'dp'=4] {'dp'}, use_global_device_ids=true, to_apply=%region_16.17 | all-reduce | flops 16384 | bytes 65536 | tf_op jit(solution)/shard_map/psum | solution.py:149
  232.6 29.7 %all-reduce.6.cloned.1.call-done = (bf16[1024,128]{1,0:T(8,128)(2,1)}, bf16[128,512]{1,0:T(8,128)(2,1)}, bf16[128,512]{1,0:T(8,128)(2,1)}) async-done(((bf16[1024,128]{1,0:T(8,128)(2,1)}, bf16[128,512]{1,0:T(8,128)(2,1)}, bf16[128,512]{1,0:T(8,128)(2,1)}), (bf16[1024,128]{1,0:T(8,128)(2,1)}, bf16[128,512]{1,0:T(8,128)(2,1)}, bf16[128,512]{1,0:T(8,128)(2,1)})) %all-reduce.6.cloned.1.call-update) | async-done | bytes 524304 | tf_op jit(solution)/shard_map/psum | solution.py:147
  262.3 1.8 convert_element_type.210
  (183 shorter events, 42.3 us)
Async XLA Ops:
  7.2 62.2 %copy-start = (bf16[1024,512]{1,0:T(8,128)(2,1)S(1)}, bf16[1024,512]{1,0:T(8,128)(2,1)}, u32[]{:S(2)}) copy-start(bf16[1024,512]{1,0:T(8,128)(2,1)} %param.15) | copy-start | bytes 3145732
  37.5 7.7 %copy-start.3 = (u32[32]{0:T(128)S(1)}, u32[32]{0:T(128)}, u32[]{:S(2)}) copy-start(u32[32]{0:T(128)} %constant.82) | copy-start | bytes 388
  37.5 9.6 %copy-start.6 = (s32[1,16]{1,0:T(1,128)S(1)}, s32[1,16]{1,0:T(1,128)}, u32[]{:S(2)}) copy-start(s32[1,16]{1,0:T(1,128)} %param.19) | copy-start | bytes 196
  38.6 21.9 %copy-start.1 = (bf16[1024,512]{1,0:T(8,128)(2,1)S(1)}, bf16[1024,512]{1,0:T(8,128)(2,1)}, u32[]{:S(2)}) copy-start(bf16[1024,512]{1,0:T(8,128)(2,1)} %param.17) | copy-start | bytes 3145732
  38.6 21.8 %all-to-all-start = ((bf16[16,128,128]{2,0,1:T(8,128)(2,1)}), bf16[16,128,128]{2,0,1:T(8,128)(2,1)S(1)}, u32[]{:S(2)}, u32[]{:S(2)}) async-start(bf16[16,128,128]{2,0,1:T(8,128)(2,1)} %copy.20), calls=%async_computation | async-start | bytes 1048576 | tf_op jit(solution)/shard_map/all_to_all | solution.py:73
  45.1 15.7 %copy-start.4 = (bf16[512,128]{1,0:T(8,128)(2,1)S(1)}, bf16[512,128]{1,0:T(8,128)(2,1)}, u32[]{:S(2)}) copy-start(bf16[512,128]{1,0:T(8,128)(2,1)} %param.18) | copy-start | bytes 393220
  45.1 79.7 %reduce-scatter.9.cloned.1.call-start = ((), (), s32[]{:S(2)}) async-start(), calls=%async_computation.7 | async-start | bytes 1179648 | tf_op jit(solution)/shard_map/reduce_scatter | solution.py:139
  60.6 9.0 %copy-start.5 = (bf16[512,128]{1,0:T(8,128)(2,1)S(1)}, bf16[512,128]{1,0:T(8,128)(2,1)}, u32[]{:S(2)}) copy-start(bf16[512,128]{1,0:T(8,128)(2,1)} %param.16) | copy-start | bytes 393220
  87.9 64.4 %reduce-scatter.5.cloned.1.call-start = ((), (), s32[]{:S(2)}) async-start(), calls=%async_computation.5 | async-start | bytes 1179648 | tf_op jit(solution)/shard_map/reduce_scatter | solution.py:133
  90.0 93.5 %reduce-scatter.11.cloned.1.call-start = ((), (), s32[]{:S(2)}) async-start(), calls=%async_computation.8 | async-start | bytes 147456 | tf_op jit(solution)/shard_map/reduce_scatter | solution.py:142
  92.7 121.9 %reduce-scatter.7.cloned.1.call-start = ((), (), s32[]{:S(2)}) async-start(), calls=%async_computation.6 | async-start | bytes 147456 | tf_op jit(solution)/shard_map/reduce_scatter | solution.py:136
  108.9 153.5 %all-reduce.6.cloned.1.call-start = ((), (), s32[]{:S(2)}) async-start(), calls=%async_computation.9 | async-start | bytes 1048576 | tf_op jit(solution)/shard_map/psum | solution.py:147
  262.3 3.4 %copy-start.2 = (bf16[128,512]{1,0:T(8,128)(2,1)S(1)}, bf16[128,512]{1,0:T(8,128)(2,1)}, u32[]{:S(2)}) copy-start(bf16[128,512]{1,0:T(8,128)(2,1)} %get-tuple-element.293) | copy-start | bytes 393220
Sparse Core Ops, SparseCore 0:
  88.0 31.0 reduce-scatter.8
  121.4 30.8 reduce-scatter.4
  155.1 28.3 reduce-scatter.10
  186.3 28.2 reduce-scatter.6
  218.1 44.1 all-reduce.5
where the time goes:
time: 274 us; the launch traced here: 273 us
  waiting for transfers between devices  123 us (45%)
  blocking collectives  66.1 us (24%)
  matrix products  48.9 us (18%)
  between operations  15.3 us (6%)
  other arithmetic  7.4 us (3%)
  starting transfers between devices  6.66 us (2%)
  local copies, waits for them, and re-layouts  4.5 us (2%)
    reduce_scatter x1, waiting for transfers between devices, shards(): lax.psum_scatter(item_head_term.astype(jnp.bfloat16), 'table', scatter_di...  31.2 us
    reduce_scatter x1, waiting for transfers between devices, shards(): lax.psum_scatter(user_head_term.astype(jnp.bfloat16), 'table', scatter_di...  31 us
    psum x1, waiting for transfers between devices, shards(): lax.psum(table_part.astype(jnp.bfloat16), 'dp').astype(jnp.float32)  29.7 us
    reduce_scatter x1, waiting for transfers between devices, shards(): lax.psum_scatter(user_layer_term.astype(jnp.bfloat16), 'table', scatter_d...  27.5 us
    dot_general x16, matrix products, pool_feature(): jnp.dot(weights, table, preferred_element_type=jnp.float32)  27.2 us
    unnamed x2, blocking collectives  25 us
    psum x1, blocking collectives, shards(): lax.psum(layer_rows[1].astype(jnp.bfloat16), 'dp').astype(jnp.float32)  16.8 us
    all_gather x1, blocking collectives, shards(): group_grads = lax.all_gather(own_grads, 'table', axis=0, tiled=True)  16.1 us
  transfers between devices with their start and end apart: 6, of which 5 were waited for; matrix products, arithmetic and copies ran while one was open for 8% of the time, Pallas kernels for 0%

commit v1 on v0

--- a/solution.py
+++ b/solution.py
@@ -1,6 +1,10 @@
+import functools
+
 import jax
 import jax.numpy as jnp
 from jax import lax
+from jax.experimental import pallas as pl
+from jax.experimental.pallas import tpu as pltpu
 from jax.sharding import PartitionSpec as P
 
 LOOKUPS = 8
@@ -45,7 +49,7 @@
     ).astype(jnp.bfloat16)
 
 
-def shards(ids, mults, table, user_layer, user_head, item_layer, item_head, counts):
+def shards_general(ids, mults, table, user_layer, user_head, item_layer, item_head, counts):
     table_count = lax.axis_size("table")
     rows_dev, emb_width = table.shape
     group_rows = ids.shape[1]
@@ -153,6 +157,405 @@
     return (losses, totals[0], totals[1], totals[2], totals[3], totals[4])
 
 
+BF16 = jnp.bfloat16
+F32 = jnp.float32
+ROW_ID = jnp.int16
+CHUNKS = 4
+MESH = pl.DeviceIdType.MESH
+
+
+def flip(value, mask, bits):
+    out = 0
+    for bit in range(bits):
+        one = lax.rem(lax.div(value, 1 << bit), 2)
+        if (mask >> bit) & 1:
+            one = 1 - one
+        out = out + one * (1 << bit)
+    return out
+
+
+def dot_nt(left, right):
+    return lax.dot_general(left, right, (((1,), (1,)), ((), ())), preferred_element_type=F32)
+
+
+def dot_tn(left, right):
+    return lax.dot_general(left, right, (((0,), (0,)), ((), ())), preferred_element_type=F32)
+
+
+def step_kernel(
+    ids_ref,
+    mults_ref,
+    table_ref,
+    user_layer_ref,
+    user_head_ref,
+    item_layer_ref,
+    item_head_ref,
+    counts_ref,
+    losses_ref,
+    table_out,
+    user_layer_out,
+    user_head_out,
+    item_layer_out,
+    item_head_out,
+    ids_t,
+    mults_t,
+    table_t,
+    row_ids,
+    weights,
+    parts,
+    pair_in,
+    sums,
+    sums_in,
+    slices,
+    slices_in,
+    units,
+    grads,
+    tower_terms,
+    tower_in,
+    tower_all,
+    table_terms,
+    table_in,
+    table_all,
+    pair_sems,
+    sums_sems,
+    slices_sems,
+    units_sems,
+    grads_sems,
+    pass_sems,
+    tower_sems,
+    tower_all_sems,
+    table_sems,
+    table_all_sems,
+):
+    t = lax.axis_index("table")
+    d = lax.axis_index("dp")
+    z = lax.div(t, 2)
+    core = lax.rem(t, 2)
+    sibling = z * 2 + (1 - core)
+    z_peers = [flip(z, k, 2) for k in range(4)]
+    dp_peers = [flip(d, k, 2) for k in range(4)]
+
+    barrier = pltpu.get_barrier_semaphore()
+    for k in range(1, 8):
+        pl.semaphore_signal(barrier, inc=1, device_id={"table": flip(t, k, 3)}, device_id_type=MESH)
+    for k in range(1, 4):
+        pl.semaphore_signal(barrier, inc=1, device_id={"dp": dp_peers[k]}, device_id_type=MESH)
+
+    def send(src, dst, sems, index, target):
+        copy = pltpu.make_async_remote_copy(
+            src_ref=src,
+            dst_ref=dst,
+            send_sem=sems.at[0, index],
+            recv_sem=sems.at[1, index],
+            device_id=target,
+            device_id_type=MESH,
+        )
+        copy.start()
+        return copy
+
+    ids_t[...] = ids_ref[...].T
+    mults_t[...] = mults_ref[...].T
+    table_t[...] = table_ref[...].T
+    row_ids[...] = lax.broadcasted_iota(jnp.int32, row_ids.shape, 0).astype(row_ids.dtype)
+    block = 128
+
+    def pool_pair(chunk, pair):
+        for half in range(2):
+            feature = chunk * 4 + pair * 2 + half
+            slots = pl.ds(pl.multiple_of(feature * 8, 8), 8)
+            id_rows = ids_t[slots, :]
+            mult_rows = mults_t[slots, :].astype(F32)
+            spread = [
+                (
+                    jnp.broadcast_to(id_rows[l : l + 1, :], (16, 128)).astype(row_ids.dtype),
+                    jnp.broadcast_to(mult_rows[l : l + 1, :], (16, 128)).astype(BF16),
+                )
+                for l in range(LOOKUPS)
+            ]
+            lanes = pl.ds(pl.multiple_of(feature * 128, 128), 128)
+            for start in range(0, 1024, block):
+                here = row_ids[start : start + block, :].reshape(block // 16, 16, 128)
+                total = None
+                for id_row, mult_row in spread:
+                    term = jnp.where(here == id_row[None], mult_row[None], jnp.zeros((), BF16))
+                    total = term if total is None else total + term
+                weights[start : start + block, lanes] = total.reshape(block, 128)
+        lanes = pl.ds(pl.multiple_of((chunk * 4 + pair * 2) * 128, 256), 256)
+        pooled_t = jnp.dot(table_t[...], weights[:, lanes], preferred_element_type=F32)
+        for half in range(2):
+            pooled = pooled_t[:, half * 128 : half * 128 + 128].T.astype(BF16)
+            place = pl.ds(pl.multiple_of((pair * 2 + half) * 128, 128), 128)
+            for owner in range(8):
+                parts[chunk, owner % 2, owner // 2, :, place] = pooled[owner * 16 : owner * 16 + 16]
+
+    pair_copies, sums_copies = [], []
+
+    def pass_on(chunk):
+        pair_copies[chunk].wait_recv()
+        total = parts[chunk, core].astype(F32) + pair_in[chunk].astype(F32)
+        sums[chunk] = total.astype(BF16)
+        for k in range(1, 4):
+            sums_copies.append(
+                send(
+                    sums.at[chunk, z_peers[k]],
+                    sums_in.at[chunk, k - 1],
+                    sums_sems,
+                    chunk * 3 + k - 1,
+                    {"table": z_peers[k] * 2 + core},
+                )
+            )
+
+    for chunk in range(CHUNKS):
+
+        def pool_step(pair, carry):
+            pool_pair(chunk, pair)
+            return carry
+
+        lax.fori_loop(0, 2, pool_step, 0)
+        if chunk == 0:
+            pl.semaphore_wait(barrier, 10)
+        pair_copies.append(
+            send(
+                parts.at[chunk, 1 - core],
+                pair_in.at[chunk],
+                pair_sems,
+                chunk,
+                {"table": sibling},
+            )
+        )
+        if chunk > 0:
+            pass_on(chunk - 1)
+    pass_on(CHUNKS - 1)
+    pooled = []
+    for chunk in range(CHUNKS):
+        total = sums[chunk, z].astype(F32)
+        for k in range(3):
+            sums_copies[chunk * 3 + k].wait_recv()
+            total = total + sums_in[chunk, k].astype(F32)
+        pooled.append(total.astype(BF16))
+    user_in = jnp.concatenate(pooled[:2], axis=1)
+    item_in = jnp.concatenate(pooled[2:], axis=1)
+
+    user_pre, user_hidden, user_unit, user_scale = run_tower(
+        user_in, user_layer_ref[...], user_head_ref[...]
+    )
+    item_pre, item_hidden, item_unit, item_scale = run_tower(
+        item_in, item_layer_ref[...], item_head_ref[...]
+    )
+    eye16 = lax.broadcasted_iota(jnp.int32, (16, 16), 0) == lax.broadcasted_iota(
+        jnp.int32, (16, 16), 1
+    )
+    count_column = jnp.sum(
+        jnp.where(eye16, jnp.broadcast_to(counts_ref[...].astype(F32), (16, 16)), 0.0),
+        axis=1,
+        keepdims=True,
+    )
+    units[0, :, 0:128] = user_unit.astype(BF16)
+    units[0, :, 128:256] = item_unit.astype(BF16)
+    units[0, :, 256:384] = jnp.broadcast_to(count_column, (16, 128)).astype(BF16)
+    units_copies = [
+        send(units.at[0], units.at[k], units_sems, k - 1, {"dp": dp_peers[k]}) for k in range(1, 4)
+    ]
+    for owner in range(8):
+        slices[owner, :, 0:128] = user_in[:, owner * 128 : owner * 128 + 128]
+        slices[owner, :, 128:256] = item_in[:, owner * 128 : owner * 128 + 128]
+        slices[owner, :, 256:384] = jnp.concatenate(
+            [
+                user_hidden[:, owner * 64 : owner * 64 + 64],
+                item_hidden[:, owner * 64 : owner * 64 + 64],
+            ],
+            axis=1,
+        )
+    slices_copies = []
+    for k in range(1, 8):
+        peer = flip(t, k, 3)
+        slices_copies.append(
+            send(slices.at[peer], slices_in.at[t], slices_sems, k - 1, {"table": peer})
+        )
+    slices_in[t] = slices[t]
+    for copy in units_copies:
+        copy.wait_recv()
+
+    every = units[...]
+    users = every[:, :, 0:128].reshape(64, 128)
+    items = every[:, :, 128:256].reshape(64, 128)
+    log_freq = jnp.log(every[:, :, 256:384].reshape(64, 128).astype(F32))[:, 0:1]
+    scores = INVERSE_TEMP * dot_nt(items, users) - log_freq
+    lse = jnp.log(jnp.sum(jnp.exp(scores), axis=0, keepdims=True))
+    same = lax.broadcasted_iota(jnp.int32, (64, 64), 0) == lax.broadcasted_iota(
+        jnp.int32, (64, 64), 1
+    )
+    positive = jnp.sum(jnp.where(same, scores, 0.0), axis=0, keepdims=True)
+    losses_ref[...] = (lse - positive)[:, 0:16]
+    dscore = (jnp.exp(scores - lse) - jnp.where(same, 1.0, 0.0)).astype(BF16)
+    d_user = INVERSE_TEMP * dot_tn(dscore, items)[0:16]
+    d_item = INVERSE_TEMP * jnp.dot(dscore[0:16], users, preferred_element_type=F32)
+
+    def back(d_unit, unit, scale, pre, head_ref):
+        along = jnp.sum(unit * d_unit, axis=-1, keepdims=True)
+        d_output = ((d_unit - unit * along) * scale).astype(BF16)
+        d_hidden = (dot_nt(d_output, head_ref[...]) * silu_slope(pre)).astype(BF16)
+        return d_output, d_hidden
+
+    user_dout, user_dhid = back(d_user, user_unit, user_scale, user_pre, user_head_ref)
+    item_dout, item_dhid = back(d_item, item_unit, item_scale, item_pre, item_head_ref)
+    grads[t] = jnp.concatenate([user_dhid, item_dhid, user_dout, item_dout], axis=1)
+    grads_copies = [
+        send(
+            grads.at[t], grads.at[t], grads_sems, k - 1, {"table": z_peers[k] * 2 + core}
+        )
+        for k in range(1, 4)
+    ]
+    pass_copies = [send(grads.at[t], grads.at[t], pass_sems, 0, {"table": sibling})]
+    for k in range(1, 4):
+        grads_copies[k - 1].wait_recv()
+        slot = z_peers[k] * 2 + core
+        pass_copies.append(
+            send(grads.at[slot], grads.at[slot], pass_sems, k, {"table": sibling})
+        )
+    for copy in pass_copies:
+        copy.wait_recv()
+    for copy in slices_copies:
+        copy.wait_recv()
+
+    every = grads[...].reshape(128, 1280)
+    kept = slices_in[...].reshape(128, 384)
+    user_rows = dot_tn(kept[:, 0:128], every[:, 0:512]).astype(BF16)
+    item_rows = dot_tn(kept[:, 128:256], every[:, 512:1024]).astype(BF16)
+    head_rows = dot_tn(kept[:, 256:384], every[:, 1024:1280]).astype(BF16)
+    for part in range(4):
+        lanes = slice(part * 128, part * 128 + 128)
+        tower_terms[part, 0:128, :] = user_rows[:, lanes]
+        tower_terms[part, 128:256, :] = item_rows[:, lanes]
+        tower_terms[part, 256:272, :] = head_rows[part * 16 : part * 16 + 16, 0:128]
+        tower_terms[part, 272:288, :] = head_rows[64 + part * 16 : 80 + part * 16, 128:256]
+    tower_copies = [
+        send(
+            tower_terms.at[dp_peers[k]], tower_in.at[k - 1], tower_sems, k - 1, {"dp": dp_peers[k]}
+        )
+        for k in range(1, 4)
+    ]
+
+    user_dpool = dot_nt(every[:, 0:512], user_layer_ref[...]).astype(BF16)
+    item_dpool = dot_nt(every[:, 512:1024], item_layer_ref[...]).astype(BF16)
+    columns = [user_dpool[:, f * 128 : f * 128 + 128] for f in range(8)] + [
+        item_dpool[:, f * 128 : f * 128 + 128] for f in range(8)
+    ]
+    d_pooled = jnp.concatenate(columns, axis=0)
+    for part in range(4):
+        table_terms[part] = jnp.dot(
+            weights[part * 256 : part * 256 + 256, :], d_pooled, preferred_element_type=F32
+        ).astype(BF16)
+    table_copies = [
+        send(
+            table_terms.at[dp_peers[k]], table_in.at[k - 1], table_sems, k - 1, {"dp": dp_peers[k]}
+        )
+        for k in range(1, 4)
+    ]
+
+    def gather_sum(terms, arrived, copies, result, sems):
+        total = terms[d].astype(F32)
+        for k in range(3):
+            copies[k].wait_recv()
+            total = total + arrived[k].astype(F32)
+        result[d] = total.astype(BF16)
+        return [
+            send(result.at[d], result.at[d], sems, k - 1, {"dp": dp_peers[k]}) for k in range(1, 4)
+        ]
+
+    tower_all_copies = gather_sum(tower_terms, tower_in, tower_copies, tower_all, tower_all_sems)
+    table_all_copies = gather_sum(table_terms, table_in, table_copies, table_all, table_all_sems)
+    for copy in tower_all_copies:
+        copy.wait_recv()
+    for part in range(4):
+        lanes = slice(part * 128, part * 128 + 128)
+        rows = slice(part * 16, part * 16 + 16)
+        user_layer_out[:, lanes] = tower_all[part, 0:128, :].astype(F32)
+        item_layer_out[:, lanes] = tower_all[part, 128:256, :].astype(F32)
+        user_head_out[rows, :] = tower_all[part, 256:272, :].astype(F32)
+        item_head_out[rows, :] = tower_all[part, 272:288, :].astype(F32)
+    for copy in table_all_copies:
+        copy.wait_recv()
+    for part in range(4):
+        table_out[part * 256 : part * 256 + 256, :] = table_all[part].astype(F32)
+    for copy in (
+        pair_copies
+        + sums_copies
+        + units_copies
+        + slices_copies
+        + grads_copies
+        + pass_copies
+        + tower_copies
+        + table_copies
+        + tower_all_copies
+        + table_all_copies
+    ):
+        copy.wait_send()
+
+
+def shards(ids, mults, table, user_layer, user_head, item_layer, item_head, counts):
+    small = lax.axis_size("table") == 8 and lax.axis_size("dp") == 4
+    if not small or ids.shape != (1, 128, 128) or table.shape != (1024, 128):
+        return shards_general(
+            ids, mults, table, user_layer, user_head, item_layer, item_head, counts
+        )
+
+    def dma(count):
+        return pltpu.SemaphoreType.DMA((2, count))
+
+    vmem = pl.BlockSpec(memory_space=pltpu.VMEM)
+    return pl.pallas_call(
+        step_kernel,
+        out_shape=(
+            jax.ShapeDtypeStruct((1, 16), F32),
+            jax.ShapeDtypeStruct((1024, 128), F32),
+            jax.ShapeDtypeStruct((128, 512), F32),
+            jax.ShapeDtypeStruct((64, 128), F32),
+            jax.ShapeDtypeStruct((128, 512), F32),
+            jax.ShapeDtypeStruct((64, 128), F32),
+        ),
+        in_specs=[vmem] * 8,
+        out_specs=(vmem,) * 6,
+        scratch_shapes=[
+            pltpu.VMEM((128, 128), jnp.int32),
+            pltpu.VMEM((128, 128), jnp.int32),
+            pltpu.VMEM((128, 1024), BF16),
+            pltpu.VMEM((1024, 128), ROW_ID),
+            pltpu.VMEM((1024, 2048), BF16),
+            pltpu.VMEM((CHUNKS, 2, 4, 16, 512), BF16),
+            pltpu.VMEM((CHUNKS, 4, 16, 512), BF16),
+            pltpu.VMEM((CHUNKS, 4, 16, 512), BF16),
+            pltpu.VMEM((CHUNKS, 3, 16, 512), BF16),
+            pltpu.VMEM((8, 16, 384), BF16),
+            pltpu.VMEM((8, 16, 384), BF16),
+            pltpu.VMEM((4, 16, 384), BF16),
+            pltpu.VMEM((8, 16, 1280), BF16),
+            pltpu.VMEM((4, 288, 128), BF16),
+            pltpu.VMEM((3, 288, 128), BF16),
+            pltpu.VMEM((4, 288, 128), BF16),
+            pltpu.VMEM((4, 256, 128), BF16),
+            pltpu.VMEM((3, 256, 128), BF16),
+            pltpu.VMEM((4, 256, 128), BF16),
+            dma(CHUNKS),
+            dma(CHUNKS * 3),
+            dma(7),
+            dma(3),
+            dma(3),
+            dma(4),
+            dma(3),
+            dma(3),
+            dma(3),
+            dma(3),
+        ],
+        compiler_params=pltpu.CompilerParams(
+            collective_id=0, has_side_effects=True, vmem_limit_bytes=40 * 1024 * 1024
+        ),
+        cost_estimate=pl.CostEstimate(
+            flops=3_000_000_000, bytes_accessed=4_500_000, transcendentals=100_000
+        ),
+    )(ids[0], mults[0], table, user_layer, user_head, item_layer, item_head, counts)
+
+
 def solution(mesh):
     in_specs = (
         P("table", "dp", None),

time: 274 us -> 56.1 us (0.20)
  waiting for transfers between devices: 123 us -> 0 us
  blocking collectives: 66.1 us -> 0 us
  matrix products: 48.9 us -> 0 us
  Pallas kernels: 0 us -> 43.6 us
  between operations: 15.3 us -> 0.66 us
  other arithmetic: 7.4 us -> 0 us
  local copies, waits for them, and re-layouts: 4.5 us -> 11.5 us
  starting transfers between devices: 6.66 us -> 0 us
    reduce_scatter x4 -> x0, waiting for transfers between devices: 89.7 us -> none  [the longest x1 31.2 us: shards(): lax.psum_scatter(item_head_term.astype(jnp.bfloat16), 'table', scatter_di...]
    dot_general x47 -> x0, matrix products: 48.9 us -> none  [the longest x16 27.2 us: pool_feature(): jnp.dot(weights, table, preferred_element_type=jnp.float32)]
    pallas_call x0 -> x1, Pallas kernels: none -> 43.6 us  [shards(): pl.pallas_call(step_kernel, out_shape=(jax.ShapeDtypeStruct((1, 16), F32)...]
    psum x1 -> x0, waiting for transfers between devices: 29.7 us -> none  [shards(): lax.psum(table_part.astype(jnp.bfloat16), 'dp').astype(jnp.float32)]
    unnamed x2 -> x0, blocking collectives: 25 us -> none
    all_gather x2 -> x0, blocking collectives: 24.3 us -> none  [the longest x1 16.1 us: shards(): group_grads = lax.all_gather(own_grads, 'table', axis=0, tiled=True)]
    psum x1 -> x0, blocking collectives: 16.8 us -> none  [shards(): lax.psum(layer_rows[1].astype(jnp.bfloat16), 'dp').astype(jnp.float32)]
    unnamed x20 -> x22, local copies, waits for them, and re-layouts: 2.84 us -> 11.5 us
  transfers between devices with their start and end apart: 6 -> 0, of which waited for: 5 -> 0; matrix products, arithmetic and copies ran while one was open for 8% -> 0% of each run, Pallas kernels for 0% -> 0%
where the time goes in v1:
time: 56.1 us; the launch traced here: 55.7 us
  Pallas kernels  43.6 us (78%)
  local copies, waits for them, and re-layouts  11.5 us (20%)
  between operations  0.66 us (1%)
    pallas_call x1, Pallas kernels, shards(): pl.pallas_call(step_kernel, out_shape=(jax.ShapeDtypeStruct((1, 16), F32)...  43.6 us
    unnamed x22, local copies, waits for them, and re-layouts  11.5 us

profile of v1, /device:TPU:0, one launch (start us, length us, event | category | flops | bytes accessed | tf_op | source)
XLA Modules:
  0.0 55.7 jit_solution(4894400121405482268)
XLA Ops:
  0.6 0.0 copy-start.7
  0.6 0.6 %copy-done.7 = s32[1,16]{1,0:T(1,128)S(1)} copy-done((s32[1,16]{1,0:T(1,128)S(1)}, s32[1,16]{1,0:T(1,128)}, u32[]{:S(2)}) %copy-start.7) | copy-done | bytes 88
  1.3 0.0 copy-start
  1.3 1.2 %copy-done = bf16[1024,512]{1,0:T(8,128)(2,1)S(1)} copy-done((bf16[1024,512]{1,0:T(8,128)(2,1)S(1)}, bf16[1024,512]{1,0:T(8,128)(2,1)}, u32[]{:S(2)}) %copy-start) | copy-done | bytes 1048600
  2.5 0.0 copy-start.1
  2.5 1.2 %copy-done.1 = bf16[1024,512]{1,0:T(8,128)(2,1)S(1)} copy-done((bf16[1024,512]{1,0:T(8,128)(2,1)S(1)}, bf16[1024,512]{1,0:T(8,128)(2,1)}, u32[]{:S(2)}) %copy-start.1) | copy-done | bytes 1048600
  3.7 0.0 copy-start.2
  3.7 0.9 %copy-done.2 = bf16[1024,128]{1,0:T(8,128)(2,1)S(1)} copy-done((bf16[1024,128]{1,0:T(8,128)(2,1)S(1)}, bf16[1024,128]{1,0:T(8,128)(2,1)}, u32[]{:S(2)}) %copy-start.2) | copy-done | bytes 262168
  4.7 0.0 copy-start.3
  4.7 0.9 %copy-done.3 = bf16[512,128]{1,0:T(8,128)(2,1)S(1)} copy-done((bf16[512,128]{1,0:T(8,128)(2,1)S(1)}, bf16[512,128]{1,0:T(8,128)(2,1)}, u32[]{:S(2)}) %copy-start.3) | copy-done | bytes 131096
  5.6 0.0 copy-start.4
  5.6 0.9 %copy-done.4 = bf16[512,128]{1,0:T(8,128)(2,1)S(1)} copy-done((bf16[512,128]{1,0:T(8,128)(2,1)S(1)}, bf16[512,128]{1,0:T(8,128)(2,1)}, u32[]{:S(2)}) %copy-start.4) | copy-done | bytes 131096
  6.5 0.0 copy-start.5
  6.5 0.8 %copy-done.5 = s32[1,128,128]{2,1,0:T(8,128)S(1)} copy-done((s32[1,128,128]{2,1,0:T(8,128)S(1)}, s32[1,128,128]{2,1,0:T(8,128)}, u32[]{:S(2)}) %copy-start.5) | copy-done | bytes 65560
  7.3 0.0 copy-start.6
  7.3 0.8 %copy-done.6 = s32[1,128,128]{2,1,0:T(8,128)S(1)} copy-done((s32[1,128,128]{2,1,0:T(8,128)S(1)}, s32[1,128,128]{2,1,0:T(8,128)}, u32[]{:S(2)}) %copy-start.6) | copy-done | bytes 65560
  8.2 43.6 %shard_map.127 = (f32[1,16]{1,0:T(1,128)S(1)}, f32[1024,128]{1,0:T(8,128)S(1)}, f32[128,512]{1,0:T(8,128)S(1)}, f32[64,128]{1,0:T(8,128)S(1)}, f32[128,512]{1,0:T(8,128)S(1)}, /*index=5*/f32[64,128]{1,0:T(8,128)S(1)}) custom-call(s32[128,128]{1,0:T(8,128)S(1)} %bitcast.2, s32[128,128]{1,0:T(8,128)S(1)} %bitcast.3, bf16[1024,128]{1,0:T(8,128)(2,1)S(1)} %copy-done.2, ...), custom_call_target="tpu_custom_call" | custom-call | flops 3000000000 | bytes 4500000 | tf_op jit(solution)/shard_map/pallas_call | solution.py:507
  51.8 0.5 copy.20
  52.3 0.8 %copy.21 = f32[1024,128]{1,0:T(8,128)} copy(f32[1024,128]{1,0:T(8,128)S(1)} %get-tuple-element.13) | data formatting | bytes 1048576
  53.1 0.7 %copy.22 = f32[128,512]{1,0:T(8,128)} copy(f32[128,512]{1,0:T(8,128)S(1)} %get-tuple-element.14) | data formatting | bytes 524288
  53.8 0.6 %copy.23 = f32[64,128]{1,0:T(8,128)} copy(f32[64,128]{1,0:T(8,128)S(1)} %get-tuple-element.15) | data formatting | bytes 65536
  54.4 0.7 %copy.24 = f32[128,512]{1,0:T(8,128)} copy(f32[128,512]{1,0:T(8,128)S(1)} %get-tuple-element.16) | data formatting | bytes 524288
  55.1 0.6 %copy.25 = f32[64,128]{1,0:T(8,128)} copy(f32[64,128]{1,0:T(8,128)S(1)} %get-tuple-element.17) | data formatting | bytes 65536
Async XLA Ops:
  0.6 0.7 %copy-start.7 = (s32[1,16]{1,0:T(1,128)S(1)}, s32[1,16]{1,0:T(1,128)}, u32[]{:S(2)}) copy-start(s32[1,16]{1,0:T(1,128)} %counts_ref.1) | copy-start | bytes 196
  1.3 1.2 %copy-start = (bf16[1024,512]{1,0:T(8,128)(2,1)S(1)}, bf16[1024,512]{1,0:T(8,128)(2,1)}, u32[]{:S(2)}) copy-start(bf16[1024,512]{1,0:T(8,128)(2,1)} %user_layer_ref.1) | copy-start | bytes 3145732
  2.5 1.2 %copy-start.1 = (bf16[1024,512]{1,0:T(8,128)(2,1)S(1)}, bf16[1024,512]{1,0:T(8,128)(2,1)}, u32[]{:S(2)}) copy-start(bf16[1024,512]{1,0:T(8,128)(2,1)} %item_layer_ref.1) | copy-start | bytes 3145732
  3.7 0.9 %copy-start.2 = (bf16[1024,128]{1,0:T(8,128)(2,1)S(1)}, bf16[1024,128]{1,0:T(8,128)(2,1)}, u32[]{:S(2)}) copy-start(bf16[1024,128]{1,0:T(8,128)(2,1)} %table_ref.1) | copy-start | bytes 786436
  4.7 0.9 %copy-start.3 = (bf16[512,128]{1,0:T(8,128)(2,1)S(1)}, bf16[512,128]{1,0:T(8,128)(2,1)}, u32[]{:S(2)}) copy-start(bf16[512,128]{1,0:T(8,128)(2,1)} %user_head_ref.1) | copy-start | bytes 393220
  5.6 0.9 %copy-start.4 = (bf16[512,128]{1,0:T(8,128)(2,1)S(1)}, bf16[512,128]{1,0:T(8,128)(2,1)}, u32[]{:S(2)}) copy-start(bf16[512,128]{1,0:T(8,128)(2,1)} %item_head_ref.1) | copy-start | bytes 393220
  6.5 0.8 %copy-start.5 = (s32[1,128,128]{2,1,0:T(8,128)S(1)}, s32[1,128,128]{2,1,0:T(8,128)}, u32[]{:S(2)}) copy-start(s32[1,128,128]{2,1,0:T(8,128)} %param.8) | copy-start | bytes 196612
  7.3 0.8 %copy-start.6 = (s32[1,128,128]{2,1,0:T(8,128)S(1)}, s32[1,128,128]{2,1,0:T(8,128)}, u32[]{:S(2)}) copy-start(s32[1,128,128]{2,1,0:T(8,128)} %param.9) | copy-start | bytes 196612

commit v2 on v1

--- a/solution.py
+++ b/solution.py
@@ -183,6 +183,17 @@
 
 
 def step_kernel(
+    ids_hbm,
+    mults_hbm,
+    table_hbm,
+    user_layer_hbm,
+    user_head_hbm,
+    item_layer_hbm,
+    item_head_hbm,
+    counts_hbm,
+    losses_ref,
+    tower_all,
+    table_all,
     ids_ref,
     mults_ref,
     table_ref,
@@ -191,12 +202,10 @@
     item_layer_ref,
     item_head_ref,
     counts_ref,
-    losses_ref,
-    table_out,
-    user_layer_out,
-    user_head_out,
-    item_layer_out,
-    item_head_out,
+    user_layer_t,
+    user_head_t,
+    item_layer_t,
+    item_head_t,
     ids_t,
     mults_t,
     table_t,
@@ -212,10 +221,9 @@
     grads,
     tower_terms,
     tower_in,
-    tower_all,
     table_terms,
     table_in,
-    table_all,
+    load_sems,
     pair_sems,
     sums_sems,
     slices_sems,
@@ -227,6 +235,19 @@
     table_sems,
     table_all_sems,
 ):
+    pairs = (
+        (ids_hbm, ids_ref),
+        (mults_hbm, mults_ref),
+        (table_hbm, table_ref),
+        (user_layer_hbm, user_layer_ref),
+        (item_layer_hbm, item_layer_ref),
+        (user_head_hbm, user_head_ref),
+        (item_head_hbm, item_head_ref),
+        (counts_hbm, counts_ref),
+    )
+    loads = [pltpu.make_async_copy(a, b, load_sems.at[i]) for i, (a, b) in enumerate(pairs)]
+    for load in loads:
+        load.start()
     t = lax.axis_index("table")
     d = lax.axis_index("dp")
     z = lax.div(t, 2)
@@ -253,10 +274,12 @@
         copy.start()
         return copy
 
+    row_ids[...] = lax.broadcasted_iota(jnp.int32, row_ids.shape, 0).astype(row_ids.dtype)
+    for load in loads[:3]:
+        load.wait()
     ids_t[...] = ids_ref[...].T
     mults_t[...] = mults_ref[...].T
     table_t[...] = table_ref[...].T
-    row_ids[...] = lax.broadcasted_iota(jnp.int32, row_ids.shape, 0).astype(row_ids.dtype)
     block = 128
 
     def pool_pair(chunk, pair):
@@ -325,7 +348,11 @@
         )
         if chunk > 0:
             pass_on(chunk - 1)
+    for load in loads[3:]:
+        load.wait()
     pass_on(CHUNKS - 1)
+    user_head_t[...] = user_head_ref[...].T
+    item_head_t[...] = item_head_ref[...].T
     pooled = []
     for chunk in range(CHUNKS):
         total = sums[chunk, z].astype(F32)
@@ -391,14 +418,16 @@
     d_user = INVERSE_TEMP * dot_tn(dscore, items)[0:16]
     d_item = INVERSE_TEMP * jnp.dot(dscore[0:16], users, preferred_element_type=F32)
 
-    def back(d_unit, unit, scale, pre, head_ref):
+    def back(d_unit, unit, scale, pre, head_t):
         along = jnp.sum(unit * d_unit, axis=-1, keepdims=True)
         d_output = ((d_unit - unit * along) * scale).astype(BF16)
-        d_hidden = (dot_nt(d_output, head_ref[...]) * silu_slope(pre)).astype(BF16)
+        d_hidden = (
+            jnp.dot(d_output, head_t[...], preferred_element_type=F32) * silu_slope(pre)
+        ).astype(BF16)
         return d_output, d_hidden
 
-    user_dout, user_dhid = back(d_user, user_unit, user_scale, user_pre, user_head_ref)
-    item_dout, item_dhid = back(d_item, item_unit, item_scale, item_pre, item_head_ref)
+    user_dout, user_dhid = back(d_user, user_unit, user_scale, user_pre, user_head_t)
+    item_dout, item_dhid = back(d_item, item_unit, item_scale, item_pre, item_head_t)
     grads[t] = jnp.concatenate([user_dhid, item_dhid, user_dout, item_dout], axis=1)
     grads_copies = [
         send(
@@ -407,6 +436,8 @@
         for k in range(1, 4)
     ]
     pass_copies = [send(grads.at[t], grads.at[t], pass_sems, 0, {"table": sibling})]
+    user_layer_t[...] = user_layer_ref[...].T
+    item_layer_t[...] = item_layer_ref[...].T
     for k in range(1, 4):
         grads_copies[k - 1].wait_recv()
         slot = z_peers[k] * 2 + core
@@ -436,8 +467,12 @@
         for k in range(1, 4)
     ]
 
-    user_dpool = dot_nt(every[:, 0:512], user_layer_ref[...]).astype(BF16)
-    item_dpool = dot_nt(every[:, 512:1024], item_layer_ref[...]).astype(BF16)
+    user_dpool = jnp.dot(
+        every[:, 0:512], user_layer_t[...], preferred_element_type=F32
+    ).astype(BF16)
+    item_dpool = jnp.dot(
+        every[:, 512:1024], item_layer_t[...], preferred_element_type=F32
+    ).astype(BF16)
     columns = [user_dpool[:, f * 128 : f * 128 + 128] for f in range(8)] + [
         item_dpool[:, f * 128 : f * 128 + 128] for f in range(8)
     ]
@@ -467,17 +502,8 @@
     table_all_copies = gather_sum(table_terms, table_in, table_copies, table_all, table_all_sems)
     for copy in tower_all_copies:
         copy.wait_recv()
-    for part in range(4):
-        lanes = slice(part * 128, part * 128 + 128)
-        rows = slice(part * 16, part * 16 + 16)
-        user_layer_out[:, lanes] = tower_all[part, 0:128, :].astype(F32)
-        item_layer_out[:, lanes] = tower_all[part, 128:256, :].astype(F32)
-        user_head_out[rows, :] = tower_all[part, 256:272, :].astype(F32)
-        item_head_out[rows, :] = tower_all[part, 272:288, :].astype(F32)
     for copy in table_all_copies:
         copy.wait_recv()
-    for part in range(4):
-        table_out[part * 256 : part * 256 + 256, :] = table_all[part].astype(F32)
     for copy in (
         pair_copies
         + sums_copies
@@ -493,6 +519,51 @@
         copy.wait_send()
 
 
+def finish_kernel(
+    losses_ref,
+    tower_ref,
+    table_ref,
+    losses_out,
+    table_out,
+    user_layer_out,
+    user_head_out,
+    item_layer_out,
+    item_head_out,
+    table_wide,
+    user_layer_wide,
+    user_head_wide,
+    item_layer_wide,
+    item_head_wide,
+    sems,
+):
+    copies = []
+
+    def put(src, dst):
+        copies.append(pltpu.make_async_copy(src, dst, sems.at[len(copies)]))
+        copies[-1].start()
+
+    put(losses_ref, losses_out)
+    for part in range(4):
+        table_wide[part * 256 : part * 256 + 256, :] = table_ref[part].astype(F32)
+    put(table_wide, table_out)
+    for part in range(4):
+        lanes = slice(part * 128, part * 128 + 128)
+        user_layer_wide[:, lanes] = tower_ref[part, 0:128, :].astype(F32)
+    put(user_layer_wide, user_layer_out)
+    for part in range(4):
+        lanes = slice(part * 128, part * 128 + 128)
+        item_layer_wide[:, lanes] = tower_ref[part, 128:256, :].astype(F32)
+    put(item_layer_wide, item_layer_out)
+    for part in range(4):
+        rows = slice(part * 16, part * 16 + 16)
+        user_head_wide[rows, :] = tower_ref[part, 256:272, :].astype(F32)
+        item_head_wide[rows, :] = tower_ref[part, 272:288, :].astype(F32)
+    put(user_head_wide, user_head_out)
+    put(item_head_wide, item_head_out)
+    for copy in copies:
+        copy.wait()
+
+
 def shards(ids, mults, table, user_layer, user_head, item_layer, item_head, counts):
     small = lax.axis_size("table") == 8 and lax.axis_size("dp") == 4
     if not small or ids.shape != (1, 128, 128) or table.shape != (1024, 128):
@@ -503,20 +574,34 @@
     def dma(count):
         return pltpu.SemaphoreType.DMA((2, count))
 
+    held = [
+        pltpu.with_memory_space_constraint(x, pltpu.HBM)
+        for x in (ids[0], mults[0], table, user_layer, user_head, item_layer, item_head, counts)
+    ]
     vmem = pl.BlockSpec(memory_space=pltpu.VMEM)
-    return pl.pallas_call(
+    hbm = pl.BlockSpec(memory_space=pltpu.HBM)
+    losses, tower_all, table_all = pl.pallas_call(
         step_kernel,
         out_shape=(
             jax.ShapeDtypeStruct((1, 16), F32),
-            jax.ShapeDtypeStruct((1024, 128), F32),
-            jax.ShapeDtypeStruct((128, 512), F32),
-            jax.ShapeDtypeStruct((64, 128), F32),
-            jax.ShapeDtypeStruct((128, 512), F32),
-            jax.ShapeDtypeStruct((64, 128), F32),
+            jax.ShapeDtypeStruct((4, 288, 128), BF16),
+            jax.ShapeDtypeStruct((4, 256, 128), BF16),
         ),
-        in_specs=[vmem] * 8,
-        out_specs=(vmem,) * 6,
+        in_specs=[hbm] * 8,
+        out_specs=(vmem,) * 3,
         scratch_shapes=[
+            pltpu.VMEM((128, 128), jnp.int32),
+            pltpu.VMEM((128, 128), jnp.int32),
+            pltpu.VMEM((1024, 128), BF16),
+            pltpu.VMEM((1024, 512), BF16),
+            pltpu.VMEM((512, 128), BF16),
+            pltpu.VMEM((1024, 512), BF16),
+            pltpu.VMEM((512, 128), BF16),
+            pltpu.VMEM((1, 16), jnp.int32),
+            pltpu.VMEM((512, 1024), BF16),
+            pltpu.VMEM((128, 512), BF16),
+            pltpu.VMEM((512, 1024), BF16),
+            pltpu.VMEM((128, 512), BF16),
             pltpu.VMEM((128, 128), jnp.int32),
             pltpu.VMEM((128, 128), jnp.int32),
             pltpu.VMEM((128, 1024), BF16),
@@ -532,10 +617,9 @@
             pltpu.VMEM((8, 16, 1280), BF16),
             pltpu.VMEM((4, 288, 128), BF16),
             pltpu.VMEM((3, 288, 128), BF16),
-            pltpu.VMEM((4, 288, 128), BF16),
             pltpu.VMEM((4, 256, 128), BF16),
             pltpu.VMEM((3, 256, 128), BF16),
-            pltpu.VMEM((4, 256, 128), BF16),
+            pltpu.SemaphoreType.DMA((8,)),
             dma(CHUNKS),
             dma(CHUNKS * 3),
             dma(7),
@@ -553,7 +637,29 @@
         cost_estimate=pl.CostEstimate(
             flops=3_000_000_000, bytes_accessed=4_500_000, transcendentals=100_000
         ),
-    )(ids[0], mults[0], table, user_layer, user_head, item_layer, item_head, counts)
+    )(*held)
+    return pl.pallas_call(
+        finish_kernel,
+        out_shape=(
+            jax.ShapeDtypeStruct((1, 16), F32),
+            jax.ShapeDtypeStruct((1024, 128), F32),
+            jax.ShapeDtypeStruct((128, 512), F32),
+            jax.ShapeDtypeStruct((64, 128), F32),
+            jax.ShapeDtypeStruct((128, 512), F32),
+            jax.ShapeDtypeStruct((64, 128), F32),
+        ),
+        in_specs=[vmem] * 3,
+        out_specs=(hbm,) * 6,
+        scratch_shapes=[
+            pltpu.VMEM((1024, 128), F32),
+            pltpu.VMEM((128, 512), F32),
+            pltpu.VMEM((64, 128), F32),
+            pltpu.VMEM((128, 512), F32),
+            pltpu.VMEM((64, 128), F32),
+            pltpu.SemaphoreType.DMA((6,)),
+        ],
+        compiler_params=pltpu.CompilerParams(vmem_limit_bytes=16 * 1024 * 1024),
+    )(losses, tower_all, table_all)
 
 
 def solution(mesh):

time: 56.1 us -> 45.9 us (0.82)
  local copies, waits for them, and re-layouts: 11.5 us -> 0 us
  Pallas kernels: 43.6 us -> 45.1 us
    unnamed x22 -> x0, local copies, waits for them, and re-layouts: 11.5 us -> none
    pallas_call x0 -> x1, Pallas kernels: none -> 1.06 us  [shards(): pl.pallas_call(finish_kernel, out_shape=(jax.ShapeDtypeStruct((1, 16), F3...]
where the time goes in v2:
time: 45.9 us; the launch traced here: 45.7 us
  Pallas kernels  45.1 us (98%)
  between operations  0.64 us (1%)
    pallas_call x1, Pallas kernels, shards(): pl.pallas_call(step_kernel, out_shape=(jax.ShapeDtypeStruct((1, 16), F32)...  44 us
    pallas_call x1, Pallas kernels, shards(): pl.pallas_call(finish_kernel, out_shape=(jax.ShapeDtypeStruct((1, 16), F3...  1.06 us

profile of v2, /device:TPU:0, one launch (start us, length us, event | category | flops | bytes accessed | tf_op | source)
XLA Modules:
  0.0 45.7 jit_solution(16625947439405948849)
XLA Ops:
  0.6 44.0 %shard_map.127 = (f32[1,16]{1,0:T(1,128)S(1)}, bf16[4,288,128]{2,1,0:T(8,128)(2,1)S(1)}, bf16[4,256,128]{2,1,0:T(8,128)(2,1)S(1)}) custom-call(s32[128,128]{1,0:T(8,128)} %bitcast.2, s32[128,128]{1,0:T(8,128)} %bitcast.3, bf16[1024,128]{1,0:T(8,128)(2,1)} %table_hbm.1, bf16[1024,512]{1,0:T(8,128)(2,1)} %user_layer_hbm.1, bf16[512,128]{1,0:T(8,128)(2,1)} %user_head_hbm.1, ...), custom_call_target="tpu_custom_call" | custom-call | flops 3000000000 | bytes 4500000 | tf_op jit(solution)/shard_map/pallas_call | solution.py:583
  44.6 1.1 %shard_map.128 = (f32[1,16]{1,0:T(1,128)}, f32[1024,128]{1,0:T(8,128)}, f32[128,512]{1,0:T(8,128)}, f32[64,128]{1,0:T(8,128)}, f32[128,512]{1,0:T(8,128)}, /*index=5*/f32[64,128]{1,0:T(8,128)}) custom-call(f32[1,16]{1,0:T(1,128)S(1)} %get-tuple-element.9.losses_ref, bf16[4,288,128]{2,1,0:T(8,128)(2,1)S(1)} %get-tuple-element.10.tower_ref, ...), custom_call_target="tpu_custom_call" | custom-call | tf_op jit(solution)/shard_map/pallas_call | solution.py:641

commit v3 on v2

--- a/solution.py
+++ b/solution.py
@@ -221,8 +221,12 @@
     grads,
     tower_terms,
     tower_in,
+    tower_mid,
+    tower_second,
     table_terms,
     table_in,
+    table_mid,
+    table_second,
     load_sems,
     pair_sems,
     sums_sems,
@@ -456,16 +460,51 @@
     head_rows = dot_tn(kept[:, 256:384], every[:, 1024:1280]).astype(BF16)
     for part in range(4):
         lanes = slice(part * 128, part * 128 + 128)
-        tower_terms[part, 0:128, :] = user_rows[:, lanes]
-        tower_terms[part, 128:256, :] = item_rows[:, lanes]
-        tower_terms[part, 256:272, :] = head_rows[part * 16 : part * 16 + 16, 0:128]
-        tower_terms[part, 272:288, :] = head_rows[64 + part * 16 : 80 + part * 16, 128:256]
-    tower_copies = [
-        send(
-            tower_terms.at[dp_peers[k]], tower_in.at[k - 1], tower_sems, k - 1, {"dp": dp_peers[k]}
-        )
-        for k in range(1, 4)
-    ]
+        tower_terms[part, 0, 0:128, :] = user_rows[:, lanes]
+        tower_terms[part, 0, 128:144, :] = head_rows[part * 16 : part * 16 + 16, 0:128]
+        tower_terms[part, 1, 0:128, :] = item_rows[:, lanes]
+        tower_terms[part, 1, 128:144, :] = head_rows[64 + part * 16 : 80 + part * 16, 128:256]
+
+    by_x, by_y, across = dp_peers[1], dp_peers[2], dp_peers[3]
+
+    def scatter_start(terms, first, sems):
+        return [
+            send(terms.at[across, 0], first.at[0, 1], sems, 0, {"dp": by_x}),
+            send(terms.at[across, 1], first.at[1, 1], sems, 1, {"dp": by_y}),
+            send(terms.at[by_x, 0], first.at[0, 0], sems, 2, {"dp": by_x}),
+            send(terms.at[by_y, 1], first.at[1, 0], sems, 3, {"dp": by_y}),
+        ]
+
+    def scatter_pass(terms, first, middle, second, copies, sems):
+        for half, target in ((0, by_y), (1, by_x)):
+            copies[half].wait_recv()
+            total = terms[target, half].astype(F32) + first[half, 1].astype(F32)
+            middle[half] = total.astype(BF16)
+            copies.append(
+                send(middle.at[half], second.at[half], sems, 4 + half, {"dp": target})
+            )
+
+    def gather_start(terms, first, second, copies, result, sems):
+        for half in range(2):
+            copies[2 + half].wait_recv()
+            copies[4 + half].wait_recv()
+            total = terms[d, half].astype(F32) + first[half, 0].astype(F32)
+            result[d, half] = (total + second[half].astype(F32)).astype(BF16)
+        own = [result.at[d, 0], result.at[d, 1]]
+        return [
+            send(own[0], own[0], sems, 0, {"dp": by_y}),
+            send(own[1], own[1], sems, 1, {"dp": by_x}),
+            send(own[0], own[0], sems, 2, {"dp": by_x}),
+            send(own[1], own[1], sems, 3, {"dp": by_y}),
+        ]
+
+    def gather_pass(copies, result, sems):
+        for half, source, target in ((0, by_y, by_x), (1, by_x, by_y)):
+            copies[half].wait_recv()
+            held = result.at[source, half]
+            copies.append(send(held, held, sems, 4 + half, {"dp": target}))
+
+    tower_copies = scatter_start(tower_terms, tower_in, tower_sems)
 
     user_dpool = jnp.dot(
         every[:, 0:512], user_layer_t[...], preferred_element_type=F32
@@ -478,31 +517,25 @@
     ]
     d_pooled = jnp.concatenate(columns, axis=0)
     for part in range(4):
-        table_terms[part] = jnp.dot(
-            weights[part * 256 : part * 256 + 256, :], d_pooled, preferred_element_type=F32
-        ).astype(BF16)
-    table_copies = [
-        send(
-            table_terms.at[dp_peers[k]], table_in.at[k - 1], table_sems, k - 1, {"dp": dp_peers[k]}
-        )
-        for k in range(1, 4)
-    ]
-
-    def gather_sum(terms, arrived, copies, result, sems):
-        total = terms[d].astype(F32)
-        for k in range(3):
-            copies[k].wait_recv()
-            total = total + arrived[k].astype(F32)
-        result[d] = total.astype(BF16)
-        return [
-            send(result.at[d], result.at[d], sems, k - 1, {"dp": dp_peers[k]}) for k in range(1, 4)
-        ]
-
-    tower_all_copies = gather_sum(tower_terms, tower_in, tower_copies, tower_all, tower_all_sems)
-    table_all_copies = gather_sum(table_terms, table_in, table_copies, table_all, table_all_sems)
-    for copy in tower_all_copies:
-        copy.wait_recv()
-    for copy in table_all_copies:
+        table_terms[part] = (
+            jnp.dot(
+                weights[part * 256 : part * 256 + 256, :], d_pooled, preferred_element_type=F32
+            )
+            .astype(BF16)
+            .reshape(2, 128, 128)
+        )
+    table_copies = scatter_start(table_terms, table_in, table_sems)
+    scatter_pass(tower_terms, tower_in, tower_mid, tower_second, tower_copies, tower_sems)
+    scatter_pass(table_terms, table_in, table_mid, table_second, table_copies, table_sems)
+    tower_all_copies = gather_start(
+        tower_terms, tower_in, tower_second, tower_copies, tower_all, tower_all_sems
+    )
+    table_all_copies = gather_start(
+        table_terms, table_in, table_second, table_copies, table_all, table_all_sems
+    )
+    gather_pass(tower_all_copies, tower_all, tower_all_sems)
+    gather_pass(table_all_copies, table_all, table_all_sems)
+    for copy in tower_all_copies[2:] + table_all_copies[2:]:
         copy.wait_recv()
     for copy in (
         pair_copies
@@ -544,20 +577,20 @@
 
     put(losses_ref, losses_out)
     for part in range(4):
-        table_wide[part * 256 : part * 256 + 256, :] = table_ref[part].astype(F32)
+        table_wide[part * 256 : part * 256 + 256, :] = table_ref[part].reshape(256, 128).astype(F32)
     put(table_wide, table_out)
     for part in range(4):
         lanes = slice(part * 128, part * 128 + 128)
-        user_layer_wide[:, lanes] = tower_ref[part, 0:128, :].astype(F32)
+        user_layer_wide[:, lanes] = tower_ref[part, 0, 0:128, :].astype(F32)
     put(user_layer_wide, user_layer_out)
     for part in range(4):
         lanes = slice(part * 128, part * 128 + 128)
-        item_layer_wide[:, lanes] = tower_ref[part, 128:256, :].astype(F32)
+        item_layer_wide[:, lanes] = tower_ref[part, 1, 0:128, :].astype(F32)
     put(item_layer_wide, item_layer_out)
     for part in range(4):
         rows = slice(part * 16, part * 16 + 16)
-        user_head_wide[rows, :] = tower_ref[part, 256:272, :].astype(F32)
-        item_head_wide[rows, :] = tower_ref[part, 272:288, :].astype(F32)
+        user_head_wide[rows, :] = tower_ref[part, 0, 128:144, :].astype(F32)
+        item_head_wide[rows, :] = tower_ref[part, 1, 128:144, :].astype(F32)
     put(user_head_wide, user_head_out)
     put(item_head_wide, item_head_out)
     for copy in copies:
@@ -584,8 +617,8 @@
         step_kernel,
         out_shape=(
             jax.ShapeDtypeStruct((1, 16), F32),
-            jax.ShapeDtypeStruct((4, 288, 128), BF16),
-            jax.ShapeDtypeStruct((4, 256, 128), BF16),
+            jax.ShapeDtypeStruct((4, 2, 144, 128), BF16),
+            jax.ShapeDtypeStruct((4, 2, 128, 128), BF16),
         ),
         in_specs=[hbm] * 8,
         out_specs=(vmem,) * 3,
@@ -615,10 +648,14 @@
             pltpu.VMEM((8, 16, 384), BF16),
             pltpu.VMEM((4, 16, 384), BF16),
             pltpu.VMEM((8, 16, 1280), BF16),
-            pltpu.VMEM((4, 288, 128), BF16),
-            pltpu.VMEM((3, 288, 128), BF16),
-            pltpu.VMEM((4, 256, 128), BF16),
-            pltpu.VMEM((3, 256, 128), BF16),
+            pltpu.VMEM((4, 2, 144, 128), BF16),
+            pltpu.VMEM((2, 2, 144, 128), BF16),
+            pltpu.VMEM((2, 144, 128), BF16),
+            pltpu.VMEM((2, 144, 128), BF16),
+            pltpu.VMEM((4, 2, 128, 128), BF16),
+            pltpu.VMEM((2, 2, 128, 128), BF16),
+            pltpu.VMEM((2, 128, 128), BF16),
+            pltpu.VMEM((2, 128, 128), BF16),
             pltpu.SemaphoreType.DMA((8,)),
             dma(CHUNKS),
             dma(CHUNKS * 3),
@@ -626,10 +663,10 @@
             dma(3),
             dma(3),
             dma(4),
-            dma(3),
-            dma(3),
-            dma(3),
-            dma(3),
+            dma(6),
+            dma(6),
+            dma(6),
+            dma(6),
         ],
         compiler_params=pltpu.CompilerParams(
             collective_id=0, has_side_effects=True, vmem_limit_bytes=40 * 1024 * 1024

time: 45.9 us -> 45.3 us (0.987)
  Pallas kernels: 45.1 us -> 44.5 us
    pallas_call x1, Pallas kernels: 44 us -> 43.4 us  [shards(): pl.pallas_call(step_kernel, out_shape=(jax.ShapeDtypeStruct((1, 16), F32)...]
where the time goes in v3:
time: 45.3 us; the launch traced here: 45.1 us
  Pallas kernels  44.5 us (98%)
  between operations  0.64 us (1%)
    pallas_call x1, Pallas kernels, shards(): pl.pallas_call(step_kernel, out_shape=(jax.ShapeDtypeStruct((1, 16), F32)...  43.4 us
    pallas_call x1, Pallas kernels, shards(): pl.pallas_call(finish_kernel, out_shape=(jax.ShapeDtypeStruct((1, 16), F3...  1.06 us

profile of v3, /device:TPU:0, one launch (start us, length us, event | category | flops | bytes accessed | tf_op | source)
XLA Modules:
  0.0 45.1 jit_solution(14998174079065812714)
XLA Ops:
  0.6 43.4 %shard_map.127 = (f32[1,16]{1,0:T(1,128)S(1)}, bf16[4,2,144,128]{3,2,1,0:T(8,128)(2,1)S(1)}, bf16[4,2,128,128]{3,2,1,0:T(8,128)(2,1)S(1)}) custom-call(s32[128,128]{1,0:T(8,128)} %bitcast.2, s32[128,128]{1,0:T(8,128)} %bitcast.3, bf16[1024,128]{1,0:T(8,128)(2,1)} %table_hbm.1, bf16[1024,512]{1,0:T(8,128)(2,1)} %user_layer_hbm.1, ...), custom_call_target="tpu_custom_call" | custom-call | flops 3000000000 | bytes 4500000 | tf_op jit(solution)/shard_map/pallas_call | solution.py:616
  44.1 1.1 %shard_map.128 = (f32[1,16]{1,0:T(1,128)}, f32[1024,128]{1,0:T(8,128)}, f32[128,512]{1,0:T(8,128)}, f32[64,128]{1,0:T(8,128)}, f32[128,512]{1,0:T(8,128)}, /*index=5*/f32[64,128]{1,0:T(8,128)}) custom-call(f32[1,16]{1,0:T(1,128)S(1)} %get-tuple-element.9.losses_ref, bf16[4,2,144,128]{3,2,1,0:T(8,128)(2,1)S(1)} %get-tuple-element.10.tower_ref, ...), custom_call_target="tpu_custom_call" | custom-call | tf_op jit(solution)/shard_map/pallas_call | solution.py:678

commit v4 on v3

--- a/solution.py
+++ b/solution.py
@@ -284,36 +284,38 @@
     ids_t[...] = ids_ref[...].T
     mults_t[...] = mults_ref[...].T
     table_t[...] = table_ref[...].T
-    block = 128
-
-    def pool_pair(chunk, pair):
-        for half in range(2):
-            feature = chunk * 4 + pair * 2 + half
-            slots = pl.ds(pl.multiple_of(feature * 8, 8), 8)
-            id_rows = ids_t[slots, :]
-            mult_rows = mults_t[slots, :].astype(F32)
-            spread = [
-                (
-                    jnp.broadcast_to(id_rows[l : l + 1, :], (16, 128)).astype(row_ids.dtype),
-                    jnp.broadcast_to(mult_rows[l : l + 1, :], (16, 128)).astype(BF16),
-                )
-                for l in range(LOOKUPS)
-            ]
-            lanes = pl.ds(pl.multiple_of(feature * 128, 128), 128)
-            for start in range(0, 1024, block):
-                here = row_ids[start : start + block, :].reshape(block // 16, 16, 128)
-                total = None
-                for id_row, mult_row in spread:
-                    term = jnp.where(here == id_row[None], mult_row[None], jnp.zeros((), BF16))
-                    total = term if total is None else total + term
-                weights[start : start + block, lanes] = total.reshape(block, 128)
-        lanes = pl.ds(pl.multiple_of((chunk * 4 + pair * 2) * 128, 256), 256)
-        pooled_t = jnp.dot(table_t[...], weights[:, lanes], preferred_element_type=F32)
+    block = 256
+
+    def build_weights(feature):
+        id_rows = ids_t[feature * 8 : feature * 8 + 8, :]
+        mult_rows = mults_t[feature * 8 : feature * 8 + 8, :].astype(F32)
+        spread = [
+            (
+                jnp.broadcast_to(id_rows[l : l + 1, :], (16, 128)).astype(row_ids.dtype),
+                jnp.broadcast_to(mult_rows[l : l + 1, :], (16, 128)).astype(BF16),
+            )
+            for l in range(LOOKUPS)
+        ]
+        for start in range(0, 1024, block):
+            here = row_ids[start : start + block, :].reshape(block // 16, 16, 128)
+            total = None
+            for id_row, mult_row in spread:
+                term = jnp.where(here == id_row[None], mult_row[None], jnp.zeros((), BF16))
+                total = term if total is None else total + term
+            weights[start : start + block, feature * 128 : feature * 128 + 128] = total.reshape(
+                block, 128
+            )
+
+    def pool_pair(pair):
+        chunk, first = pair // 2, pair % 2 * 2
+        pooled_t = jnp.dot(
+            table_t[...], weights[:, pair * 256 : pair * 256 + 256], preferred_element_type=F32
+        )
         for half in range(2):
             pooled = pooled_t[:, half * 128 : half * 128 + 128].T.astype(BF16)
-            place = pl.ds(pl.multiple_of((pair * 2 + half) * 128, 128), 128)
+            lanes = slice((first + half) * 128, (first + half) * 128 + 128)
             for owner in range(8):
-                parts[chunk, owner % 2, owner // 2, :, place] = pooled[owner * 16 : owner * 16 + 16]
+                parts[chunk, owner % 2, owner // 2, :, lanes] = pooled[owner * 16 : owner * 16 + 16]
 
     pair_copies, sums_copies = [], []
 
@@ -332,13 +334,29 @@
                 )
             )
 
-    for chunk in range(CHUNKS):
-
-        def pool_step(pair, carry):
-            pool_pair(chunk, pair)
-            return carry
-
-        lax.fori_loop(0, 2, pool_step, 0)
+    def pooled_chunk(chunk):
+        total = sums[chunk, z].astype(F32)
+        for k in range(3):
+            sums_copies[chunk * 3 + k].wait_recv()
+            total = total + sums_in[chunk, k].astype(F32)
+        return total.astype(BF16)
+
+    def tower_out(pre, head):
+        hidden = jax.nn.silu(pre).astype(BF16)
+        output = jnp.dot(hidden, head, preferred_element_type=F32)
+        scale = lax.rsqrt(jnp.sum(output * output, axis=-1, keepdims=True) + EPSILON)
+        return hidden, output * scale, scale
+
+    build_weights(0)
+    build_weights(1)
+    for pair in range(8):
+        pool_pair(pair)
+        if pair < 7:
+            build_weights(pair * 2 + 2)
+            build_weights(pair * 2 + 3)
+        if pair % 2 == 0:
+            continue
+        chunk = pair // 2
         if chunk == 0:
             pl.semaphore_wait(barrier, 10)
         pair_copies.append(
@@ -354,25 +372,21 @@
             pass_on(chunk - 1)
     for load in loads[3:]:
         load.wait()
+
+    user_in = jnp.concatenate([pooled_chunk(0), pooled_chunk(1)], axis=1)
+    user_pre = jnp.dot(user_in, user_layer_ref[...], preferred_element_type=F32)
     pass_on(CHUNKS - 1)
+    user_hidden, user_unit, user_scale = tower_out(user_pre, user_head_ref[...])
     user_head_t[...] = user_head_ref[...].T
     item_head_t[...] = item_head_ref[...].T
-    pooled = []
-    for chunk in range(CHUNKS):
-        total = sums[chunk, z].astype(F32)
-        for k in range(3):
-            sums_copies[chunk * 3 + k].wait_recv()
-            total = total + sums_in[chunk, k].astype(F32)
-        pooled.append(total.astype(BF16))
-    user_in = jnp.concatenate(pooled[:2], axis=1)
-    item_in = jnp.concatenate(pooled[2:], axis=1)
-
-    user_pre, user_hidden, user_unit, user_scale = run_tower(
-        user_in, user_layer_ref[...], user_head_ref[...]
-    )
-    item_pre, item_hidden, item_unit, item_scale = run_tower(
-        item_in, item_layer_ref[...], item_head_ref[...]
-    )
+    item_first = pooled_chunk(2)
+    item_pre = jnp.dot(item_first, item_layer_ref[0:512, :], preferred_element_type=F32)
+    item_last = pooled_chunk(3)
+    item_in = jnp.concatenate([item_first, item_last], axis=1)
+    item_pre = item_pre + jnp.dot(
+        item_last, item_layer_ref[512:1024, :], preferred_element_type=F32
+    )
+    item_hidden, item_unit, item_scale = tower_out(item_pre, item_head_ref[...])
     eye16 = lax.broadcasted_iota(jnp.int32, (16, 16), 0) == lax.broadcasted_iota(
         jnp.int32, (16, 16), 1
     )

time: 45.3 us -> 48.8 us (1.077)
  Pallas kernels: 44.5 us -> 48 us
    pallas_call x1, Pallas kernels: 43.4 us -> 46.9 us  [shards(): pl.pallas_call(step_kernel, out_shape=(jax.ShapeDtypeStruct((1, 16), F32)...]
where the time goes in v4:
time: 48.8 us; the launch traced here: 48.6 us
  Pallas kernels  48 us (98%)
  between operations  0.64 us (1%)
    pallas_call x1, Pallas kernels, shards(): pl.pallas_call(step_kernel, out_shape=(jax.ShapeDtypeStruct((1, 16), F32)...  46.9 us
    pallas_call x1, Pallas kernels, shards(): pl.pallas_call(finish_kernel, out_shape=(jax.ShapeDtypeStruct((1, 16), F3...  1.06 us

profile of v4, /device:TPU:0, one launch (start us, length us, event | category | flops | bytes accessed | tf_op | source)
XLA Modules:
  0.0 48.6 jit_solution(8687719090625418753)
XLA Ops:
  0.6 46.9 %shard_map.127 = (f32[1,16]{1,0:T(1,128)S(1)}, bf16[4,2,144,128]{3,2,1,0:T(8,128)(2,1)S(1)}, bf16[4,2,128,128]{3,2,1,0:T(8,128)(2,1)S(1)}) custom-call(s32[128,128]{1,0:T(8,128)} %bitcast.2, s32[128,128]{1,0:T(8,128)} %bitcast.3, bf16[1024,128]{1,0:T(8,128)(2,1)} %table_hbm.1, bf16[1024,512]{1,0:T(8,128)(2,1)} %user_layer_hbm.1, ...), custom_call_target="tpu_custom_call" | custom-call | flops 3000000000 | bytes 4500000 | tf_op jit(solution)/shard_map/pallas_call | solution.py:630
  47.5 1.1 %shard_map.128 = (f32[1,16]{1,0:T(1,128)}, f32[1024,128]{1,0:T(8,128)}, f32[128,512]{1,0:T(8,128)}, f32[64,128]{1,0:T(8,128)}, f32[128,512]{1,0:T(8,128)}, /*index=5*/f32[64,128]{1,0:T(8,128)}) custom-call(f32[1,16]{1,0:T(1,128)S(1)} %get-tuple-element.9.losses_ref, bf16[4,2,144,128]{3,2,1,0:T(8,128)(2,1)S(1)} %get-tuple-element.10.tower_ref, ...), custom_call_target="tpu_custom_call" | custom-call | tf_op jit(solution)/shard_map/pallas_call | solution.py:692

commit v5 on v4

--- a/solution.py
+++ b/solution.py
@@ -227,6 +227,7 @@
     table_in,
     table_mid,
     table_second,
+    pooled_grads,
     load_sems,
     pair_sems,
     sums_sems,
@@ -287,8 +288,10 @@
     block = 256
 
     def build_weights(feature):
-        id_rows = ids_t[feature * 8 : feature * 8 + 8, :]
-        mult_rows = mults_t[feature * 8 : feature * 8 + 8, :].astype(F32)
+        slots = pl.ds(pl.multiple_of(feature * 8, 8), 8)
+        lanes = pl.ds(pl.multiple_of(feature * 128, 128), 128)
+        id_rows = ids_t[slots, :]
+        mult_rows = mults_t[slots, :].astype(F32)
         spread = [
             (
                 jnp.broadcast_to(id_rows[l : l + 1, :], (16, 128)).astype(row_ids.dtype),
@@ -296,48 +299,64 @@
             )
             for l in range(LOOKUPS)
         ]
-        for start in range(0, 1024, block):
-            here = row_ids[start : start + block, :].reshape(block // 16, 16, 128)
+
+        def block_step(part, carry):
+            rows = pl.ds(pl.multiple_of(part * block, block), block)
+            here = row_ids[rows, :].reshape(block // 16, 16, 128)
             total = None
             for id_row, mult_row in spread:
                 term = jnp.where(here == id_row[None], mult_row[None], jnp.zeros((), BF16))
                 total = term if total is None else total + term
-            weights[start : start + block, feature * 128 : feature * 128 + 128] = total.reshape(
-                block, 128
-            )
-
-    def pool_pair(pair):
-        chunk, first = pair // 2, pair % 2 * 2
-        pooled_t = jnp.dot(
-            table_t[...], weights[:, pair * 256 : pair * 256 + 256], preferred_element_type=F32
-        )
-        for half in range(2):
-            pooled = pooled_t[:, half * 128 : half * 128 + 128].T.astype(BF16)
-            lanes = slice((first + half) * 128, (first + half) * 128 + 128)
+            weights[rows, lanes] = total.reshape(block, 128)
+            return carry
+
+        lax.fori_loop(0, 1024 // block, block_step, 0)
+
+    def pool_chunk(chunk):
+        lanes = pl.ds(pl.multiple_of(chunk * 512, 512), 512)
+        pooled_t = jnp.dot(table_t[...], weights[:, lanes], preferred_element_type=F32)
+        for at in range(4):
+            pooled = pooled_t[:, at * 128 : at * 128 + 128].T.astype(BF16)
             for owner in range(8):
-                parts[chunk, owner % 2, owner // 2, :, lanes] = pooled[owner * 16 : owner * 16 + 16]
-
-    pair_copies, sums_copies = [], []
+                parts[chunk, owner % 2, owner // 2, :, at * 128 : at * 128 + 128] = pooled[
+                    owner * 16 : owner * 16 + 16
+                ]
+
+    def remote(src, dst, sems, index, target):
+        return pltpu.make_async_remote_copy(
+            src_ref=src,
+            dst_ref=dst,
+            send_sem=sems.at[0, index],
+            recv_sem=sems.at[1, index],
+            device_id=target,
+            device_id_type=MESH,
+        )
+
+    def pair_copy(chunk):
+        return remote(
+            parts.at[chunk, 1 - core], pair_in.at[chunk], pair_sems, chunk, {"table": sibling}
+        )
+
+    def sums_copy(chunk, k):
+        return remote(
+            sums.at[chunk, z_peers[k]],
+            sums_in.at[chunk, k - 1],
+            sums_sems,
+            chunk * 3 + k - 1,
+            {"table": z_peers[k] * 2 + core},
+        )
 
     def pass_on(chunk):
-        pair_copies[chunk].wait_recv()
+        pair_copy(chunk).wait_recv()
         total = parts[chunk, core].astype(F32) + pair_in[chunk].astype(F32)
         sums[chunk] = total.astype(BF16)
         for k in range(1, 4):
-            sums_copies.append(
-                send(
-                    sums.at[chunk, z_peers[k]],
-                    sums_in.at[chunk, k - 1],
-                    sums_sems,
-                    chunk * 3 + k - 1,
-                    {"table": z_peers[k] * 2 + core},
-                )
-            )
+            sums_copy(chunk, k).start()
 
     def pooled_chunk(chunk):
         total = sums[chunk, z].astype(F32)
         for k in range(3):
-            sums_copies[chunk * 3 + k].wait_recv()
+            sums_copy(chunk, k + 1).wait_recv()
             total = total + sums_in[chunk, k].astype(F32)
         return total.astype(BF16)
 
@@ -347,29 +366,24 @@
         scale = lax.rsqrt(jnp.sum(output * output, axis=-1, keepdims=True) + EPSILON)
         return hidden, output * scale, scale
 
-    build_weights(0)
-    build_weights(1)
-    for pair in range(8):
-        pool_pair(pair)
-        if pair < 7:
-            build_weights(pair * 2 + 2)
-            build_weights(pair * 2 + 3)
-        if pair % 2 == 0:
-            continue
-        chunk = pair // 2
-        if chunk == 0:
-            pl.semaphore_wait(barrier, 10)
-        pair_copies.append(
-            send(
-                parts.at[chunk, 1 - core],
-                pair_in.at[chunk],
-                pair_sems,
-                chunk,
-                {"table": sibling},
-            )
-        )
-        if chunk > 0:
+    pl.semaphore_wait(barrier, 10)
+
+    def chunk_step(chunk, carry):
+        def feature_step(at, inner):
+            build_weights(chunk * 4 + at)
+            return inner
+
+        lax.fori_loop(0, 4, feature_step, 0)
+        pool_chunk(chunk)
+        pair_copy(chunk).start()
+
+        @pl.when(chunk > 0)
+        def _():
             pass_on(chunk - 1)
+
+        return carry
+
+    lax.fori_loop(0, CHUNKS, chunk_step, 0)
     for load in loads[3:]:
         load.wait()
 
@@ -454,8 +468,14 @@
         for k in range(1, 4)
     ]
     pass_copies = [send(grads.at[t], grads.at[t], pass_sems, 0, {"table": sibling})]
-    user_layer_t[...] = user_layer_ref[...].T
-    item_layer_t[...] = item_layer_ref[...].T
+
+    def turn(part, carry):
+        rows = pl.ds(pl.multiple_of(part * 128, 128), 128)
+        user_layer_t[:, rows] = user_layer_ref[rows, :].T
+        item_layer_t[:, rows] = item_layer_ref[rows, :].T
+        return carry
+
+    lax.fori_loop(0, 8, turn, 0)
     for k in range(1, 4):
         grads_copies[k - 1].wait_recv()
         slot = z_peers[k] * 2 + core
@@ -530,14 +550,15 @@
         item_dpool[:, f * 128 : f * 128 + 128] for f in range(8)
     ]
     d_pooled = jnp.concatenate(columns, axis=0)
-    for part in range(4):
-        table_terms[part] = (
-            jnp.dot(
-                weights[part * 256 : part * 256 + 256, :], d_pooled, preferred_element_type=F32
-            )
-            .astype(BF16)
-            .reshape(2, 128, 128)
-        )
+    pooled_grads[...] = d_pooled
+
+    def table_step(part, carry):
+        rows = pl.ds(pl.multiple_of(part * 512, 512), 512)
+        terms = jnp.dot(weights[rows, :], pooled_grads[...], preferred_element_type=F32)
+        table_terms[pl.ds(part * 2, 2)] = terms.astype(BF16).reshape(2, 2, 128, 128)
+        return carry
+
+    lax.fori_loop(0, 2, table_step, 0)
     table_copies = scatter_start(table_terms, table_in, table_sems)
     scatter_pass(tower_terms, tower_in, tower_mid, tower_second, tower_copies, tower_sems)
     scatter_pass(table_terms, table_in, table_mid, table_second, table_copies, table_sems)
@@ -552,8 +573,8 @@
     for copy in tower_all_copies[2:] + table_all_copies[2:]:
         copy.wait_recv()
     for copy in (
-        pair_copies
-        + sums_copies
+        [pair_copy(chunk) for chunk in range(CHUNKS)]
+        + [sums_copy(chunk, k) for chunk in range(CHUNKS) for k in range(1, 4)]
         + units_copies
         + slices_copies
         + grads_copies
@@ -670,6 +691,7 @@
             pltpu.VMEM((2, 2, 128, 128), BF16),
             pltpu.VMEM((2, 128, 128), BF16),
             pltpu.VMEM((2, 128, 128), BF16),
+            pltpu.VMEM((2048, 128), BF16),
             pltpu.SemaphoreType.DMA((8,)),
             dma(CHUNKS),
             dma(CHUNKS * 3),

time: 48.8 us -> 46.7 us (0.957)
  Pallas kernels: 48 us -> 45.9 us
    pallas_call x1, Pallas kernels: 46.9 us -> 44.9 us  [shards(): pl.pallas_call(step_kernel, out_shape=(jax.ShapeDtypeStruct((1, 16), F32)...]
where the time goes in v5:
time: 46.7 us; the launch traced here: 46.6 us
  Pallas kernels  45.9 us (98%)
  between operations  0.64 us (1%)
    pallas_call x1, Pallas kernels, shards(): pl.pallas_call(step_kernel, out_shape=(jax.ShapeDtypeStruct((1, 16), F32)...  44.9 us
    pallas_call x1, Pallas kernels, shards(): pl.pallas_call(finish_kernel, out_shape=(jax.ShapeDtypeStruct((1, 16), F3...  1.06 us

profile of v5, /device:TPU:0, one launch (start us, length us, event | category | flops | bytes accessed | tf_op | source)
XLA Modules:
  0.0 46.6 jit_solution(1084110945742936274)
XLA Ops:
  0.6 44.9 %shard_map.127 = (f32[1,16]{1,0:T(1,128)S(1)}, bf16[4,2,144,128]{3,2,1,0:T(8,128)(2,1)S(1)}, bf16[4,2,128,128]{3,2,1,0:T(8,128)(2,1)S(1)}) custom-call(s32[128,128]{1,0:T(8,128)} %bitcast.2, s32[128,128]{1,0:T(8,128)} %bitcast.3, bf16[1024,128]{1,0:T(8,128)(2,1)} %table_hbm.1, bf16[1024,512]{1,0:T(8,128)(2,1)} %user_layer_hbm.1, ...), custom_call_target="tpu_custom_call" | custom-call | flops 3000000000 | bytes 4500000 | tf_op jit(solution)/shard_map/pallas_call | solution.py:651
  45.5 1.1 %shard_map.128 = (f32[1,16]{1,0:T(1,128)}, f32[1024,128]{1,0:T(8,128)}, f32[128,512]{1,0:T(8,128)}, f32[64,128]{1,0:T(8,128)}, f32[128,512]{1,0:T(8,128)}, /*index=5*/f32[64,128]{1,0:T(8,128)}) custom-call(f32[1,16]{1,0:T(1,128)S(1)} %get-tuple-element.9.losses_ref, bf16[4,2,144,128]{3,2,1,0:T(8,128)(2,1)S(1)} %get-tuple-element.10.tower_ref, ...), custom_call_target="tpu_custom_call" | custom-call | tf_op jit(solution)/shard_map/pallas_call | solution.py:714

commit v6 on v3

--- a/solution.py
+++ b/solution.py
@@ -355,21 +355,19 @@
     for load in loads[3:]:
         load.wait()
     pass_on(CHUNKS - 1)
-    user_head_t[...] = user_head_ref[...].T
-    item_head_t[...] = item_head_ref[...].T
-    pooled = []
-    for chunk in range(CHUNKS):
+
+    def pooled_chunk(chunk):
         total = sums[chunk, z].astype(F32)
         for k in range(3):
             sums_copies[chunk * 3 + k].wait_recv()
             total = total + sums_in[chunk, k].astype(F32)
-        pooled.append(total.astype(BF16))
-    user_in = jnp.concatenate(pooled[:2], axis=1)
-    item_in = jnp.concatenate(pooled[2:], axis=1)
-
+        return total.astype(BF16)
+
+    user_in = jnp.concatenate([pooled_chunk(0), pooled_chunk(1)], axis=1)
     user_pre, user_hidden, user_unit, user_scale = run_tower(
         user_in, user_layer_ref[...], user_head_ref[...]
     )
+    item_in = jnp.concatenate([pooled_chunk(2), pooled_chunk(3)], axis=1)
     item_pre, item_hidden, item_unit, item_scale = run_tower(
         item_in, item_layer_ref[...], item_head_ref[...]
     )
@@ -404,6 +402,8 @@
             send(slices.at[peer], slices_in.at[t], slices_sems, k - 1, {"table": peer})
         )
     slices_in[t] = slices[t]
+    user_head_t[...] = user_head_ref[...].T
+    item_head_t[...] = item_head_ref[...].T
     for copy in units_copies:
         copy.wait_recv()
 

time: 45.3 us -> 45 us (level)
  no operation moved by 1% of the time
where the time goes in v6:
time: 45 us; the launch traced here: 44.8 us
  Pallas kernels  44.2 us (98%)
  between operations  0.64 us (1%)
    pallas_call x1, Pallas kernels, shards(): pl.pallas_call(step_kernel, out_shape=(jax.ShapeDtypeStruct((1, 16), F32)...  43.1 us
    pallas_call x1, Pallas kernels, shards(): pl.pallas_call(finish_kernel, out_shape=(jax.ShapeDtypeStruct((1, 16), F3...  1.06 us

profile of v6, /device:TPU:0, one launch (start us, length us, event | category | flops | bytes accessed | tf_op | source)
XLA Modules:
  0.0 44.8 jit_solution(14761567421092314780)
XLA Ops:
  0.6 43.1 %shard_map.127 = (f32[1,16]{1,0:T(1,128)S(1)}, bf16[4,2,144,128]{3,2,1,0:T(8,128)(2,1)S(1)}, bf16[4,2,128,128]{3,2,1,0:T(8,128)(2,1)S(1)}) custom-call(s32[128,128]{1,0:T(8,128)} %bitcast.2, s32[128,128]{1,0:T(8,128)} %bitcast.3, bf16[1024,128]{1,0:T(8,128)(2,1)} %table_hbm.1, bf16[1024,512]{1,0:T(8,128)(2,1)} %user_layer_hbm.1, ...), custom_call_target="tpu_custom_call" | custom-call | flops 3000000000 | bytes 4500000 | tf_op jit(solution)/shard_map/pallas_call | solution.py:616
  43.8 1.1 %shard_map.128 = (f32[1,16]{1,0:T(1,128)}, f32[1024,128]{1,0:T(8,128)}, f32[128,512]{1,0:T(8,128)}, f32[64,128]{1,0:T(8,128)}, f32[128,512]{1,0:T(8,128)}, /*index=5*/f32[64,128]{1,0:T(8,128)}) custom-call(f32[1,16]{1,0:T(1,128)S(1)} %get-tuple-element.9.losses_ref, bf16[4,2,144,128]{3,2,1,0:T(8,128)(2,1)S(1)} %get-tuple-element.10.tower_ref, ...), custom_call_target="tpu_custom_call" | custom-call | tf_op jit(solution)/shard_map/pallas_call | solution.py:678
